TPU v7x, 512 devices: a whole 4x4x16 slice. The times are simulated.
512 devices in a mesh: rep: 64 (over z_lo, x, core), gz: 8 (over z_hi, y).
Axes of the slice: x: 4, y: 4, z: 16 (z_hi: 2, z_lo: 8; z = z_hi * 8 + z_lo), core: 2. Of those that a mesh axis runs over, the one named last changes fastest.
Arguments:
- layer_input: bfloat16 [64, 16, 32, 16, 128], P('rep', 'gz'), may hold values from -6 to 6
- pre_act: bfloat16 [64, 16, 32, 16, 128], P('rep', 'gz'), may hold values from -6 to 6
- cotangent: bfloat16 [64, 16, 32, 16, 128], P('rep', 'gz'), may hold values from -6 to 6
- w_one: bfloat16 [27, 128, 128], replicated, may hold values from -0.109375 to 0.109375
- w_two: bfloat16 [27, 128, 128], replicated, may hold values from -0.109375 to 0.109375
Outputs:
- input_grad: bfloat16 [64, 16, 32, 16, 128], P('rep', 'gz')
- grad_one: float32 [3456, 128], P('rep', 'gz')
- grad_two: float32 [3456, 128], P('rep', 'gz')
All inputs are finite; a program needn't handle non-finite values.
Results may differ from a plain program's by a relative error of at most 0.015.
Values may be sent and summed in bfloat16 or wider, within the bound.
A program may use at most 64 MiB of HBM per device.

v0:
```python
import math

import jax
import jax.numpy as jnp
from jax import lax
from jax.sharding import PartitionSpec as P

leak_slope = 0.3


def with_halo(cells, sides, width):
    for axis, dim in sides:
        count = lax.axis_size(axis)
        ends = count - 1
        head = lax.slice_in_dim(cells, 0, width, axis=dim)
        tail = lax.slice_in_dim(cells, cells.shape[dim] - width, cells.shape[dim], axis=dim)
        cells = jnp.concatenate(
            [
                lax.ppermute(tail, axis, [(i, (i + 1) % count) for i in range(ends)]),
                cells,
                lax.ppermute(head, axis, [((i + 1) % count, i) for i in range(ends)]),
            ],
            axis=dim,
        )
    return cells


def data_grad(padded_z, kernel):
    width = kernel.shape[-1]
    flipped = kernel.reshape(3, 3, 3, width, width)[::-1, ::-1, ::-1].transpose(0, 1, 2, 4, 3)
    return lax.conv_general_dilated(
        padded_z,
        flipped,
        (1, 1, 1),
        [(0, 0), (1, 1), (1, 1)],
        dimension_numbers=("NDHWC", "DHWIO", "NDHWC"),
        preferred_element_type=jnp.float32,
    )


def weight_grad(padded_z, grad):
    width = grad.shape[-1]
    full = jnp.pad(padded_z, ((0, 0), (0, 0), (1, 1), (1, 1), (0, 0)))
    planes, rows, cols = (grad.shape[1], grad.shape[2], grad.shape[3])
    flat = grad.reshape(-1, width)
    blocks = []
    for step_z in range(3):
        for step_y in range(3):
            for step_x in range(3):
                piece = full[
                    :, step_z : step_z + planes, step_y : step_y + rows, step_x : step_x + cols, :
                ].reshape(-1, width)
                blocks.append(
                    lax.dot_general(
                        piece, flat, (((0,), (0,)), ((), ())), preferred_element_type=jnp.float32
                    )
                )
    return jnp.stack(blocks).reshape(-1, width)


def reduce_grad(terms):
    partial_sum = lax.psum_scatter(
        terms.astype(jnp.bfloat16), "gz", scatter_dimension=1, tiled=True
    ).astype(jnp.float32)
    return lax.psum_scatter(partial_sum, "rep", scatter_dimension=0, tiled=True)


def on_device(layer_input, pre_act, cotangent, w_one, w_two):
    local_cells = (
        layer_input.shape[0] * layer_input.shape[1] * layer_input.shape[2] * layer_input.shape[3]
    )
    factor = 1.0 / math.sqrt(local_cells * lax.axis_size("rep") * lax.axis_size("gz"))
    pre_f = pre_act.astype(jnp.float32)
    act = jnp.where(pre_f > 0, pre_f, leak_slope * pre_f).astype(jnp.bfloat16)
    stacked = jnp.stack([layer_input, act, cotangent])
    extended = with_halo(stacked, (("gz", 2),), 1)
    input_ext = extended[0]
    act_ext = extended[1]
    cot_ext = extended[2]
    grad_two = reduce_grad(weight_grad(act_ext, cotangent) * factor)
    act_grad = data_grad(cot_ext, w_two)
    pre_grad = (act_grad * jnp.where(pre_f > 0, 1.0, leak_slope)).astype(jnp.bfloat16)
    grad_ext = with_halo(pre_grad, (("gz", 1),), 1)
    grad_one = reduce_grad(weight_grad(input_ext, pre_grad) * factor)
    input_grad = data_grad(grad_ext, w_one).astype(jnp.bfloat16)
    return (input_grad, grad_one, grad_two)


def solution(mesh):
    in_specs = (
        P("rep", "gz", None, None, None),
        P("rep", "gz", None, None, None),
        P("rep", "gz", None, None, None),
        P(),
        P(),
    )
    out_specs = (P("rep", "gz", None, None, None), P("rep", "gz"), P("rep", "gz"))
    return jax.shard_map(
        on_device, mesh=mesh, in_specs=in_specs, out_specs=out_specs, check_vma=False
    )
```

profile of v0, /device:TPU:24, one launch (start us, length us, event | category | flops | bytes accessed | tf_op | source)
XLA Modules:
  0.0 734.1 jit_solution(12139014850367842450)
XLA Ops:
  7.2 1.1 fusion.84
  8.3 1.2 copy_bitcast_fusion
  9.7 15.4 %collective-permute-start = (bf16[3,1,1,32,16,128]{5,3,4,2,1,0:T(8,128)(2,1)S(1)}, bf16[3,1,1,32,16,128]{5,3,4,2,1,0:T(8,128)(2,1)S(1)}, u32[]{:S(2)}, u32[]{:S(2)}) collective-permute-start(bf16[3,1,1,32,16,128]{5,3,4,2,1,0:T(8,128)(2,1)S(1)} %get-tuple-element.14), channel_id=1, source_target_pairs={{0,1},{1,2},{2,3},{3,4},{4,5},{5,6},{6,7},{8,9},{9,10},{10,11},{11... | collective-permute-start | bytes 1179656 | tf_op jit(solution)/shard_map/ppermute | solution.py:19
  25.1 1.9 collective-permute-start.1
  27.0 6.4 collective-permute-done
  33.4 15.2 %collective-permute-done.1 = bf16[3,1,1,32,16,128]{5,3,4,2,1,0:T(8,128)(2,1)S(1)} collective-permute-done((bf16[3,1,1,32,16,128]{5,3,4,2,1,0:T(8,128)(2,1)S(1)}, bf16[3,1,1,32,16,128]{5,3,4,2,1,0:T(8,128)(2,1)S(1)}, u32[]{:S(2)}, u32[]{:S(2)}) %collective-permute-start.1) | collective-permute-done | bytes 393248 | tf_op jit(solution)/shard_map/ppermute | solution.py:21
  48.9 0.3 slice_bitcast_fusion
  49.2 0.7 copy-done.2
  49.8 0.3 fusion.51
  50.1 0.3 fusion.50
  50.4 0.3 fusion.49
  51.5 0.3 fusion.45
  51.8 0.3 fusion.44
  52.0 0.3 fusion.43
  52.3 0.3 fusion.42
  52.6 0.3 fusion.41
  52.9 0.3 fusion.40
  53.7 0.3 fusion.37
  53.9 0.3 fusion.36
  54.2 0.3 fusion.35
  54.8 0.3 fusion.33
  55.0 0.3 fusion.32
  55.3 0.3 fusion.31
  56.1 0.3 fusion.28
  56.4 0.3 fusion.27
  56.7 0.3 fusion.26
  57.0 0.3 fusion.25
  57.5 1.7 copy.116
  59.5 0.3 copy.83
  60.1 3.0 fusion.22
  63.4 0.3 fusion.78
  63.7 0.3 fusion.77
  64.0 0.3 fusion.76
  64.8 0.3 fusion.73
  65.1 0.3 fusion.72
  65.3 0.3 fusion.71
  65.6 0.3 fusion.70
  65.9 0.3 fusion.69
  66.2 0.3 fusion.68
  66.4 0.3 fusion.67
  67.3 0.3 fusion.64
  67.5 0.3 fusion.63
  67.8 0.3 fusion.62
  68.1 0.3 fusion.61
  68.4 0.3 fusion.60
  68.7 0.3 fusion.59
  68.9 0.3 fusion.58
  70.0 0.3 fusion.54
  70.3 0.3 fusion.53
  70.6 0.3 fusion.52
  71.1 1.7 copy.88
  72.9 1.9 collective-permute-start.2
  74.8 4.1 collective-permute-start.3
  79.0 1.3 dynamic-slice
  80.9 11.6 %collective-permute-done.3 = bf16[1,1,32,16,128]{4,2,3,1,0:T(8,128)(2,1)S(1)} collective-permute-done((bf16[1,1,32,16,128]{4,2,3,1,0:T(8,128)(2,1)S(1)}, bf16[1,1,32,16,128]{4,2,3,1,0:T(8,128)(2,1)S(1)}, u32[]{:S(2)}, u32[]{:S(2)}) %collective-permute-start.3) | collective-permute-done | bytes 131104 | tf_op jit(solution)/shard_map/ppermute | solution.py:21
  92.7 0.3 copy.86
  93.1 0.6 copy-done.3
  93.7 2.9 fusion.19
  96.8 0.8 copy.117
  97.6 96.5 %reduce-scatter.7.cloned.1.call-done = bf16[3456,16]{0,1:T(8,128)(2,1)} async-done(((bf16[3456,128]{0,1:T(8,128)(2,1)}), bf16[3456,16]{0,1:T(8,128)(2,1)}) %reduce-scatter.7.cloned.1.call-update) | async-done | bytes 110608 | tf_op jit(solution)/shard_map/reduce_scatter | solution.py:62
  194.1 109.7 %reduce-scatter.5.cloned.1.call-done = bf16[3456,16]{0,1:T(8,128)(2,1)} async-done(((bf16[3456,128]{0,1:T(8,128)(2,1)}), bf16[3456,16]{0,1:T(8,128)(2,1)}) %reduce-scatter.5.cloned.1.call-update) | async-done | bytes 110608 | tf_op jit(solution)/shard_map/reduce_scatter | solution.py:62
  303.7 422.2 %all-reduce.6 = (f32[3456,16]{0,1:T(8,128)S(1)}, f32[3456,16]{0,1:T(8,128)S(1)}) all-reduce(bf16[3456,16]{0,1:T(8,128)(2,1)} %reduce-scatter.5.cloned.1.call-done, bf16[3456,16]{0,1:T(8,128)(2,1)} %reduce-scatter.7.cloned.1.call-done), channel_id=3, replica_groups=mesh['rep'=64,'gz'=8] {'rep'}, use_global_device_ids=true, to_apply=%region_1.2.clone | all-reduce | flops 110592 | bytes 663552
  725.9 0.7 constant_dynamic-slice_fusion
  726.6 0.7 constant_dynamic-slice_fusion.1
  (43 shorter events, 6.1 us)
Async XLA Ops:
  7.2 52.8 %copy-start = (bf16[27,128,128]{2,1,0:T(8,128)(2,1)S(1)}, bf16[27,128,128]{2,1,0:T(8,128)(2,1)}, u32[]{:S(2)}) copy-start(bf16[27,128,128]{2,1,0:T(8,128)(2,1)} %param.9) | copy-start | bytes 2654212
  7.2 186.9 %reduce-scatter.7.cloned.1.call-start = ((), (), s32[]{:S(2)}) async-start(), calls=%async_computation.3 | async-start | bytes 995328 | tf_op jit(solution)/shard_map/reduce_scatter | solution.py:62
  9.7 23.7 %collective-permute-start = (bf16[3,1,1,32,16,128]{5,3,4,2,1,0:T(8,128)(2,1)S(1)}, bf16[3,1,1,32,16,128]{5,3,4,2,1,0:T(8,128)(2,1)S(1)}, u32[]{:S(2)}, u32[]{:S(2)}) collective-permute-start(bf16[3,1,1,32,16,128]{5,3,4,2,1,0:T(8,128)(2,1)S(1)} %get-tuple-element.14), channel_id=1, source_target_pairs={{0,1},{1,2},{2,3},{3,4},{4,5},{5,6},{6,7},{8,9},{9,10},{10,11},{11... | collective-permute-start | bytes 1179656 | tf_op jit(solution)/shard_map/ppermute | solution.py:19
  25.1 23.6 %collective-permute-start.1 = (bf16[3,1,1,32,16,128]{5,3,4,2,1,0:T(8,128)(2,1)S(1)}, bf16[3,1,1,32,16,128]{5,3,4,2,1,0:T(8,128)(2,1)S(1)}, u32[]{:S(2)}, u32[]{:S(2)}) collective-permute-start(bf16[3,1,1,32,16,128]{5,3,4,2,1,0:T(8,128)(2,1)S(1)} %get-tuple-element.15), channel_id=1, source_target_pairs={{1,0},{2,1},{3,2},{4,3},{5,4},{6,5},{7,6},{9,8},{10,9},{11,10},{12... | collective-permute-start | bytes 1179656 | tf_op jit(solution)/shard_map/ppermute | solution.py:21
  48.9 1.0 copy-start.2
  59.2 244.6 %reduce-scatter.5.cloned.1.call-start = ((), (), s32[]{:S(2)}) async-start(), calls=%async_computation.2 | async-start | bytes 995328 | tf_op jit(solution)/shard_map/reduce_scatter | solution.py:62
  59.4 0.7 copy-start.4
  60.1 3.2 copy-start.1
  72.9 8.0 %collective-permute-start.2 = (bf16[1,1,32,16,128]{4,2,3,1,0:T(8,128)(2,1)S(1)}, bf16[1,1,32,16,128]{4,2,3,1,0:T(8,128)(2,1)S(1)}, u32[]{:S(2)}, u32[]{:S(2)}) collective-permute-start(bf16[1,1,32,16,128]{4,2,3,1,0:T(8,128)(2,1)S(1)} %get-tuple-element.16), channel_id=1, source_target_pairs={{0,1},{1,2},{2,3},{3,4},{4,5},{5,6},{6,7},{8,9},{9,10},{10,11},{11... | collective-permute-start | bytes 393224 | tf_op jit(solution)/shard_map/ppermute | solution.py:19
  74.8 17.7 %collective-permute-start.3 = (bf16[1,1,32,16,128]{4,2,3,1,0:T(8,128)(2,1)S(1)}, bf16[1,1,32,16,128]{4,2,3,1,0:T(8,128)(2,1)S(1)}, u32[]{:S(2)}, u32[]{:S(2)}) collective-permute-start(bf16[1,1,32,16,128]{4,2,3,1,0:T(8,128)(2,1)S(1)} %get-tuple-element.17), channel_id=1, source_target_pairs={{1,0},{2,1},{3,2},{4,3},{5,4},{6,5},{7,6},{9,8},{10,9},{11,10},{12... | collective-permute-start | bytes 393224 | tf_op jit(solution)/shard_map/ppermute | solution.py:21
  92.6 1.2 copy-start.3
Sparse Core Ops, SparseCore 0:
  59.3 134.7 reduce-scatter.6
  199.3 104.3 reduce-scatter.4
where the time goes:
time: 735 us; the launch traced here: 734 us
  blocking collectives  422 us (57%)
  waiting for transfers between devices  239 us (33%)
  starting transfers between devices  23.6 us (3%)
  matrix products  20.4 us (3%)
  between operations  15.3 us (2%)
  local copies, waits for them, and re-layouts  11 us (1%)
    unnamed x1, blocking collectives  422 us
    reduce_scatter x2, waiting for transfers between devices, reduce_grad(): lax.psum_scatter(terms.astype(jnp.bfloat16), 'gz', scatter_dimension=1, t...  206 us
    ppermute x2, waiting for transfers between devices, with_halo(): lax.ppermute(head, axis, [((i + 1) % count, i) for i in range(ends)])  26.8 us
    ppermute x2, starting transfers between devices, with_halo(): lax.ppermute(tail, axis, [(i, (i + 1) % count) for i in range(ends)])  17.3 us
  transfers between devices with their start and end apart: 6, of which 5 were waited for; matrix products, arithmetic and copies ran while one was open for 3% of the time, Pallas kernels for 0%

commit v1 on v0

v1 whole, which is shorter than its diff:
```python
import functools
import math

import jax
import jax.numpy as jnp
from jax import lax
from jax.experimental import pallas as pl
from jax.experimental.pallas import tpu as pltpu
from jax.sharding import PartitionSpec as P

leak_slope = 0.3
MESH = pl.DeviceIdType.MESH
BF = jnp.bfloat16
F32 = jnp.float32

CH = 128
ROW = 16
EDGE = 32
PLANE = EDGE * ROW
PAD = PLANE + 2 * ROW
PART = PLANE // 8


def remote(src, dst, ssem, rsem, dev):
    return pltpu.make_async_remote_copy(
        src_ref=src, dst_ref=dst, send_sem=ssem, recv_sem=rsem, device_id=dev, device_id_type=MESH
    )


class Halo:
    def __init__(self, rep, g, low, high, halo, relay, ss, rs):
        self.rep, self.g = rep, g
        self.far = lax.rem(rep + 32, 64)
        self.low, self.high, self.halo, self.relay, self.ss, self.rs = low, high, halo, relay, ss, rs

    def up(self):
        return remote(self.high, self.halo.at[0], self.ss.at[0], self.rs.at[0], (self.rep, self.g + 1))

    def down(self):
        return remote(self.low, self.halo.at[1], self.ss.at[1], self.rs.at[1], (self.rep, self.g - 1))

    def part(self, side, k):
        src = self.high if side == 0 else self.low
        return remote(
            src.at[pl.ds(k * PART, PART)],
            self.relay.at[side],
            self.ss.at[2 + k],
            self.rs.at[2 + side],
            (self.far, k),
        )

    def pass_on(self, side):
        return remote(
            self.relay.at[side],
            self.halo.at[side, pl.ds(pl.multiple_of(self.g * PART, PART), PART)],
            self.ss.at[10 + side],
            self.rs.at[4 + self.g],
            (self.far, 4 - side),
        )

    def landed(self, side, k):
        block = self.halo.at[side, pl.ds(k * PART, PART)]
        return remote(block, block, self.ss.at[2 + k], self.rs.at[4 + k], (self.far, k))

    def send_high(self):
        @pl.when((self.g != 3) & (self.g != 7))
        def _():
            self.up().start()

        @pl.when(self.g == 3)
        def _():
            for k in range(8):
                self.part(0, k).start()

    def send_low(self):
        @pl.when((self.g != 0) & (self.g != 4))
        def _():
            self.down().start()

        @pl.when(self.g == 4)
        def _():
            for k in range(8):
                self.part(1, k).start()

    def forward(self):
        for side in (0, 1):
            copy = remote(
                self.relay.at[side], self.relay.at[side], self.ss.at[10], self.rs.at[2 + side], (self.far, 3)
            )
            copy.wait_recv()
            self.pass_on(side).start()

    def wait_low(self):
        @pl.when((self.g != 0) & (self.g != 4))
        def _():
            self.up().wait_recv()

        @pl.when(self.g == 4)
        def _():
            for k in range(8):
                self.landed(0, k).wait_recv()

    def wait_high(self):
        @pl.when((self.g != 3) & (self.g != 7))
        def _():
            self.down().wait_recv()

        @pl.when(self.g == 3)
        def _():
            for k in range(8):
                self.landed(1, k).wait_recv()

    def drain(self):
        @pl.when((self.g != 3) & (self.g != 7))
        def _():
            self.up().wait_send()

        @pl.when((self.g != 0) & (self.g != 4))
        def _():
            self.down().wait_send()

        @pl.when(self.g == 3)
        def _():
            for k in range(8):
                self.part(0, k).wait_send()

        @pl.when(self.g == 4)
        def _():
            for k in range(8):
                self.part(1, k).wait_send()

        for side in (0, 1):
            self.pass_on(side).wait_send()


class Where:
    def __init__(self):
        self.rep, self.g = lax.axis_index("rep"), lax.axis_index("gz")
        self.core = lax.rem(self.rep, 2)
        self.x = lax.rem(lax.div(self.rep, 2), 4)
        self.zl = lax.div(self.rep, 8)
        self.y = lax.rem(self.g, 4)
        self.zh = lax.div(self.g, 4)
        self.z = self.zh * 8 + self.zl

    def other_core(self):
        return (self.rep + 1 - 2 * self.core, self.g)

    def at_x(self, d):
        x = lax.rem(self.x + d, 4)
        return x, (self.zl * 8 + x * 2 + self.core, self.g)

    def at_y(self, d):
        y = lax.rem(self.y + d, 4)
        return y, (self.rep, self.zh * 4 + y)

    def at_z(self, d):
        z = lax.rem(self.z + d, 16)
        rest = self.rep - self.zl * 8
        return z, (lax.rem(z, 8) * 8 + rest, lax.div(z, 8) * 4 + self.y)


class Reduce:
    def __init__(self, w, s, rc, t, r1, u, r2, zs, rz, ss, rs):
        self.w = w
        self.s, self.rc, self.t, self.r1, self.u = s, rc, t, r1, u
        self.r2, self.zs, self.rz, self.ss, self.rs = r2, zs, rz, ss, rs

    def core_copy(self):
        return remote(
            self.s.at[1 - self.w.core], self.rc, self.ss.at[0], self.rs.at[0], self.w.other_core()
        )

    def first(self, half, d):
        place, dev = self.w.at_x(d) if half == 0 else self.w.at_y(d)
        k = 1 + half * 3 + d - 1
        return remote(self.t.at[half, place], self.r1.at[half, d - 1], self.ss.at[k], self.rs.at[k], dev)

    def second(self, half, d):
        place, dev = self.w.at_y(d) if half == 0 else self.w.at_x(d)
        k = 7 + half * 3 + d - 1
        return remote(self.u.at[half, place], self.r2.at[half, d - 1], self.ss.at[k], self.rs.at[k], dev)

    def last(self, d):
        place, dev = self.w.at_z(d)
        k = 13 + d - 1
        return remote(self.zs.at[place], self.rz.at[d - 1], self.ss.at[k], self.rs.at[k], dev)

    def start(self):
        self.core_copy().start()

    def step_core(self):
        self.core_copy().wait_recv()
        core = self.w.core
        for half in range(2):

            def body(i, carry):
                for j in range(4):
                    own = self.s[core, half, i, j].astype(F32)
                    self.t[half, i, j] = (own + self.rc[half, i, j].astype(F32)).astype(BF)
                return carry

            lax.fori_loop(0, 4, body, 0)
            for d in (2, 1, 3):
                self.first(half, d).start()

    def step_first(self):
        for half in range(2):
            mine = self.w.x if half == 0 else self.w.y
            for d in (1, 3, 2):
                self.first(half, d).wait_recv()

            def body(i, carry):
                total = self.t[half, mine, i].astype(F32)
                for k in range(3):
                    total += self.r1[half, k, i].astype(F32)
                self.u[half, i] = total.astype(BF)
                return carry

            lax.fori_loop(0, 4, body, 0)
            for d in (2, 1, 3):
                self.second(half, d).start()

    def step_second(self):
        for half in range(2):
            mine = self.w.y if half == 0 else self.w.x
            for d in (1, 3, 2):
                self.second(half, d).wait_recv()
            total = self.u[half, mine].astype(F32)
            for k in range(3):
                total += self.r2[half, k].astype(F32)
            self.zs[half * 8 : half * 8 + 8] = total.reshape(8, 8, CH)
        for d in (8, 7, 9, 6, 10, 5, 11, 4, 12, 3, 13, 2, 14, 1, 15):
            self.last(d).start()

    def finish(self, out, factor):
        total = self.zs[self.w.z]
        for d in (1, 15, 2, 14, 3, 13, 4, 12, 5, 11, 6, 10, 7, 9, 8):
            self.last(d).wait_recv()
            total += self.rz[d - 1]
        total = total * factor
        for q in range(8):
            piece = total if q == 0 else pltpu.roll(total, CH - 16 * q, 1)
            rows = 7 if q < 7 else 5
            out[7 * q : 7 * q + rows, :] = piece[:rows, :16]

    def drain(self):
        self.core_copy().wait_send()
        for half in range(2):
            for d in (1, 2, 3):
                self.first(half, d).wait_send()
                self.second(half, d).wait_send()
        for d in range(1, 16):
            self.last(d).wait_send()


def regroup(flat, s):
    group = lax.broadcasted_iota(jnp.int32, (8, CH), 1)
    masks = {b: lax.rem(lax.div(group, 16 * b), 2) == 1 for b in (1, 2, 4)}

    def body(pair, carry):
        block = flat.at[pl.ds(pl.multiple_of(pair * 864, 8), 872)]
        for x in range(4):
            for core in range(2):
                tiles = []
                for odd in range(2):
                    base = odd * 432 + x * 108 + core * 54
                    v = [block[base + 7 * q : base + 7 * q + 8, :] for q in range(8)]
                    for b in (1, 2, 4):
                        for q in range(8):
                            if q & b:
                                continue
                            a, c = v[q], v[q | b]
                            v[q] = jnp.where(masks[b], pltpu.roll(c, 16 * b, 1), a)
                            v[q | b] = jnp.where(masks[b], c, pltpu.roll(a, CH - 16 * b, 1))
                    tiles.append(v)
                rows = pl.ds(pl.multiple_of(pair * 16, 16), 16)
                for q in range(8):
                    both = jnp.concatenate([tiles[0][q], tiles[1][q]], axis=0).astype(BF)
                    if q < 4:
                        s[core, 0, x, q, rows, :] = both
                    else:
                        s[core, 1, q - 4, x, rows, :] = both
        return carry

    lax.fori_loop(0, 4, body, 0)


def spread(plane, ext, at):
    wide = plane.astype(F32)
    col = lax.rem(lax.broadcasted_iota(jnp.int32, (PLANE, CH), 0), ROW)
    before = jnp.where(col == 0, 0.0, pltpu.roll(wide, 1, 0)).astype(BF)
    after = jnp.where(col == ROW - 1, 0.0, pltpu.roll(wide, PLANE - 1, 0)).astype(BF)
    rows = slice(ROW, ROW + PLANE)
    ext[at, rows, 0:CH] = before
    ext[at, rows, CH : 2 * CH] = plane
    ext[at, rows, 2 * CH : 3 * CH] = after


def slabs(ext, at):
    return jnp.concatenate([ext[at, dy * ROW : dy * ROW + PLANE, :] for dy in range(3)], axis=1)


def mm(a, b):
    return jnp.dot(a, b, preferred_element_type=F32)


def lay_weights(w, wt):
    for a in range(3):
        for dy in range(3):
            for dx in range(3):
                k = dy * 3 + dx
                wt[a, k * CH : (k + 1) * CH, :] = w[9 * a + 8 - k].T


def inner_data_grad(ext, wt, acc):
    for at in (1, 2):
        x = slabs(ext, at)
        pair = jnp.concatenate([wt[2 - at], wt[3 - at]], axis=1)
        if at == 1:
            acc[...] = mm(x, pair)
        else:
            acc[...] += mm(x, pair)


def kernel(
    factor, li_h, pa_h, ct_h, w1_h, w2_h, ig, g1, g2,
    li, pa, ct, w1, w2, ct_halo, li_halo, pg_halo, ct_relay, li_relay, pg_relay,
    e_ct, e_pg, pg, act_t, li_t, wt2, wt1, acc, flat,
    s1, rc1, t1, r11, u1, r21, zs1, rz1, s2, rc2, t2, r12, u2, r22, zs2, rz2,
    in_sem, hs_ct, hr_ct, hs_li, hr_li, hs_pg, hr_pg, ss1, rs1, ss2, rs2,
):
    w = Where()
    rep, g = w.rep, w.g
    loads = [
        pltpu.make_async_copy(a, b, in_sem.at[k])
        for k, (a, b) in enumerate([(ct_h, ct), (w2_h, w2), (pa_h, pa), (li_h, li), (w1_h, w1)])
    ]
    for load in loads:
        load.start()

    barrier = pltpu.get_barrier_semaphore()
    peers = [w.other_core()]
    peers += [w.at_x(d)[1] for d in (1, 2, 3)] + [w.at_y(d)[1] for d in (1, 2, 3)]
    peers += [w.at_z(d)[1] for d in range(1, 16)]
    far = lax.rem(rep + 32, 64)
    peers += [(far, 3), (far, 4)]
    for dev in peers:
        pl.semaphore_signal(barrier, inc=1, device_id=dev, device_id_type=MESH)
    middle = (g == 3) | (g == 4)

    @pl.when(middle)
    def _():
        for k in range(8):
            pl.semaphore_signal(barrier, inc=1, device_id=(far, k), device_id_type=MESH)

    @pl.when(middle)
    def _():
        pl.semaphore_wait(barrier, len(peers) + 8)

    @pl.when(jnp.logical_not(middle))
    def _():
        pl.semaphore_wait(barrier, len(peers))

    low, high = pl.ds(0, PLANE), pl.ds(PLANE, PLANE)
    loads[0].wait()
    h_ct = Halo(rep, g, ct.at[low], ct.at[high], ct_halo, ct_relay, hs_ct, hr_ct)
    h_ct.send_high()
    h_ct.send_low()
    loads[3].wait()
    h_li = Halo(rep, g, li.at[low], li.at[high], li_halo, li_relay, hs_li, hr_li)
    h_li.send_high()
    h_li.send_low()
    h_pg = Halo(rep, g, pg.at[low], pg.at[high], pg_halo, pg_relay, hs_pg, hr_pg)

    @pl.when(g == 0)
    def _():
        for halo in (ct_halo, li_halo, pg_halo):
            halo[0] = jnp.zeros((PLANE, CH), BF)

    @pl.when(g == 7)
    def _():
        for halo in (ct_halo, li_halo, pg_halo):
            halo[1] = jnp.zeros((PLANE, CH), BF)

    edge = jnp.zeros((4, ROW, 3 * CH), BF)
    for ext in (e_ct, e_pg):
        ext[:, 0:ROW, :] = edge
        ext[:, ROW + PLANE : PAD, :] = edge
    flat[27 * CH : 27 * CH + 8, :] = jnp.zeros((8, CH), F32)
    spread(ct[low, :], e_ct, 1)
    spread(ct[high, :], e_ct, 2)
    loads[1].wait()
    lay_weights(w2, wt2)
    h_ct.forward()
    inner_data_grad(e_ct, wt2, acc)
    loads[2].wait()
    for q in range(2):
        v = pa[q * PLANE : (q + 1) * PLANE, :].astype(F32)
        act = jnp.where(v > 0, v, leak_slope * v).astype(BF)
        act_t[:, q * PLANE : (q + 1) * PLANE] = act.T
    h_li.forward()

    h_ct.wait_low()
    spread(ct_halo[0], e_ct, 0)
    h_ct.wait_high()
    spread(ct_halo[1], e_ct, 3)
    for q in range(2):
        total = acc[:, q * CH : (q + 1) * CH] + mm(slabs(e_ct, 3 * q), wt2[2 - 2 * q])
        rows = pl.ds(q * PLANE, PLANE)
        v = pa[rows, :].astype(F32)
        pg[rows, :] = (total * jnp.where(v > 0, 1.0, leak_slope)).astype(BF)
        if q == 0:
            h_pg.send_low()
        else:
            h_pg.send_high()

    order = [(0, 1), (2, 3), (4, 5), (6, 7), (8,)]

    def taps(ext, at, group):
        parts = []
        for k in group:
            dy, dx = 2 - k // 3, 2 - k % 3
            parts.append(ext[at, dy * ROW : dy * ROW + PLANE, dx * CH : (dx + 1) * CH])
        return parts[0] if len(parts) == 1 else jnp.concatenate(parts, axis=1)

    a0, a1 = act_t[:, 0:PLANE], act_t[:, PLANE : 2 * PLANE]
    for group in order:
        e = [taps(e_ct, at, group) for at in range(4)]
        mid = mm(jnp.concatenate([a0, a1], axis=0), e[1])
        after = mm(jnp.concatenate([a0, a1], axis=0), e[2])
        planes = [
            after[:CH] + mm(a1, e[3]),
            mid[:CH] + after[CH:],
            mid[CH:] + mm(a0, e[0]),
        ]
        for a in range(3):
            for j, k in enumerate(group):
                t = 9 * a + k
                flat[t * CH : (t + 1) * CH, :] = planes[a][:, j * CH : (j + 1) * CH]
    red2 = Reduce(w, s2, rc2, t2, r12, u2, r22, zs2, rz2, ss2, rs2)
    regroup(flat, s2)
    red2.start()
    h_pg.forward()

    spread(pg[low, :], e_pg, 1)
    spread(pg[high, :], e_pg, 2)
    li_t[:, PLANE : 2 * PLANE] = li[low, :].T
    li_t[:, 2 * PLANE : 3 * PLANE] = li[high, :].T
    h_li.wait_low()
    li_t[:, 0:PLANE] = li_halo[0].T
    h_li.wait_high()
    li_t[:, 3 * PLANE : 4 * PLANE] = li_halo[1].T
    red2.step_core()
    for group in order:
        total = None
        for at in (1, 2):
            lhs = jnp.concatenate(
                [li_t[:, (at + a - 1) * PLANE : (at + a) * PLANE] for a in range(3)], axis=0
            )
            term = mm(lhs, taps(e_pg, at, group))
            total = term if total is None else total + term
        for a in range(3):
            for j, k in enumerate(group):
                t = 9 * a + k
                flat[t * CH : (t + 1) * CH, :] = total[a * CH : (a + 1) * CH, j * CH : (j + 1) * CH]
    red1 = Reduce(w, s1, rc1, t1, r11, u1, r21, zs1, rz1, ss1, rs1)
    regroup(flat, s1)
    red1.start()
    red2.step_first()

    loads[4].wait()
    lay_weights(w1, wt1)
    red1.step_core()
    red2.step_second()
    inner_data_grad(e_pg, wt1, acc)
    h_pg.wait_low()
    spread(pg_halo[0], e_pg, 0)
    h_pg.wait_high()
    spread(pg_halo[1], e_pg, 3)
    red1.step_first()
    red2.finish(g2, factor)
    for q in range(2):
        total = acc[:, q * CH : (q + 1) * CH] + mm(slabs(e_pg, 3 * q), wt1[2 - 2 * q])
        ig[q * PLANE : (q + 1) * PLANE, :] = total.astype(BF)
        if q == 0:
            red1.step_second()
    red1.finish(g1, factor)

    for halo in (h_ct, h_li, h_pg):
        halo.drain()
    red2.drain()
    red1.drain()


def reduce_buffers():
    return [
        pltpu.VMEM((2, 2, 4, 4, 64, CH), BF),
        pltpu.VMEM((2, 4, 4, 64, CH), BF),
        pltpu.VMEM((2, 4, 4, 64, CH), BF),
        pltpu.VMEM((2, 3, 4, 64, CH), BF),
        pltpu.VMEM((2, 4, 64, CH), BF),
        pltpu.VMEM((2, 3, 64, CH), BF),
        pltpu.VMEM((16, 8, CH), F32),
        pltpu.VMEM((15, 8, CH), F32),
    ]


def on_device(layer_input, pre_act, cotangent, w_one, w_two):
    shape = layer_input.shape
    cells = 2 * PLANE
    factor = 1.0 / math.sqrt(cells * lax.axis_size("rep") * lax.axis_size("gz"))
    flat_in = [v.reshape(cells, CH) for v in (layer_input, pre_act, cotangent)]
    any_spec = pl.BlockSpec(memory_space=pl.ANY)
    vmem_spec = pl.BlockSpec(memory_space=pltpu.VMEM)
    dma = pltpu.SemaphoreType.DMA
    field = pltpu.VMEM((cells, CH), BF)
    kern = pltpu.VMEM((27, CH, CH), BF)
    halo = pltpu.VMEM((2, PLANE, CH), BF)
    relay = pltpu.VMEM((2, PART, CH), BF)
    ext = pltpu.VMEM((4, PAD, 3 * CH), BF)
    turned = pltpu.VMEM((3, 9 * CH, CH), BF)
    input_grad, grad_one, grad_two = pl.pallas_call(
        functools.partial(kernel, factor),
        out_shape=(
            jax.ShapeDtypeStruct((cells, CH), BF),
            jax.ShapeDtypeStruct((54, 16), F32),
            jax.ShapeDtypeStruct((54, 16), F32),
        ),
        in_specs=[any_spec] * 5,
        out_specs=(vmem_spec, vmem_spec, vmem_spec),
        scratch_shapes=[
            field, field, field, kern, kern, halo, halo, halo, relay, relay, relay,
            ext, ext, field, pltpu.VMEM((CH, cells), BF), pltpu.VMEM((CH, 2 * cells), BF),
            turned, turned, pltpu.VMEM((PLANE, 2 * CH), F32), pltpu.VMEM((27 * CH + 8, CH), F32),
            *reduce_buffers(), *reduce_buffers(),
            dma((5,)), *[dma((12,))] * 6, *[dma((28,))] * 4,
        ],
        compiler_params=pltpu.CompilerParams(
            collective_id=0, has_side_effects=True, vmem_limit_bytes=48 * 2**20
        ),
    )(*flat_in, w_one, w_two)
    return (input_grad.reshape(shape), grad_one, grad_two)


def solution(mesh):
    cells = P("rep", "gz", None, None, None)
    return jax.shard_map(
        on_device,
        mesh=mesh,
        in_specs=(cells, cells, cells, P(), P()),
        out_specs=(cells, P("rep", "gz"), P("rep", "gz")),
        check_vma=False,
    )
```

time: 735 us -> 81.4 us (0.11)
  the two profiles are of different devices: /device:TPU:24 before, /device:TPU:32 now
where the time goes in v1:
time: 81.4 us; the launch traced here: 81.1 us
  Pallas kernels  73.3 us (90%)
  local copies, waits for them, and re-layouts  7.22 us (9%)
    pallas_call x1, Pallas kernels, on_device(): pl.pallas_call(functools.partial(kernel, factor), out_shape=(jax.ShapeDty...  73.3 us
    unnamed x13, local copies, waits for them, and re-layouts  7.22 us

profile of v1, /device:TPU:32, one launch (start us, length us, event | category | flops | bytes accessed | tf_op | source)
XLA Modules:
  0.0 81.1 jit_solution(11678476513910082412)
XLA Ops:
  0.6 0.0 copy-start
  0.6 1.2 %copy-done = bf16[27,128,128]{2,1,0:T(8,128)(2,1)S(1)} copy-done((bf16[27,128,128]{2,1,0:T(8,128)(2,1)S(1)}, bf16[27,128,128]{2,1,0:T(8,128)(2,1)}, u32[]{:S(2)}) %copy-start) | copy-done | bytes 884760
  1.8 0.0 copy-start.1
  1.8 1.2 %copy-done.1 = bf16[27,128,128]{2,1,0:T(8,128)(2,1)S(1)} copy-done((bf16[27,128,128]{2,1,0:T(8,128)(2,1)S(1)}, bf16[27,128,128]{2,1,0:T(8,128)(2,1)}, u32[]{:S(2)}) %copy-start.1) | copy-done | bytes 884760
  3.0 0.0 copy-start.2
  3.0 0.9 %copy-done.2 = bf16[1,2,32,16,128]{4,3,2,1,0:T(8,128)(2,1)S(1)} copy-done((bf16[1,2,32,16,128]{4,3,2,1,0:T(8,128)(2,1)S(1)}, bf16[1,2,32,16,128]{4,3,2,1,0:T(8,128)(2,1)}, u32[]{:S(2)}) %copy-start.2) | copy-done | bytes 262168
  3.9 0.0 copy-start.3
  3.9 0.9 %copy-done.3 = bf16[1,2,32,16,128]{4,3,2,1,0:T(8,128)(2,1)S(1)} copy-done((bf16[1,2,32,16,128]{4,3,2,1,0:T(8,128)(2,1)S(1)}, bf16[1,2,32,16,128]{4,3,2,1,0:T(8,128)(2,1)}, u32[]{:S(2)}) %copy-start.3) | copy-done | bytes 262168
  4.9 0.0 copy-start.4
  4.9 0.9 %copy-done.4 = bf16[1,2,32,16,128]{4,3,2,1,0:T(8,128)(2,1)S(1)} copy-done((bf16[1,2,32,16,128]{4,3,2,1,0:T(8,128)(2,1)S(1)}, bf16[1,2,32,16,128]{4,3,2,1,0:T(8,128)(2,1)}, u32[]{:S(2)}) %copy-start.4) | copy-done | bytes 262168
  5.8 73.3 %shard_map.76 = (bf16[1024,128]{1,0:T(8,128)(2,1)S(1)}, f32[54,16]{1,0:T(8,128)S(1)}, f32[54,16]{1,0:T(8,128)S(1)}) custom-call(bf16[1024,128]{1,0:T(8,128)(2,1)S(1)} %bitcast.4, bf16[1024,128]{1,0:T(8,128)(2,1)S(1)} %bitcast.5, bf16[1024,128]{1,0:T(8,128)(2,1)S(1)} %bitcast.6, bf16[27,128,128]{2,1,0:T(8,128)(2,1)S(1)} %copy-done, ...), custom_call_target="tpu_custom_call" | custom-call | tf_op jit(solution)/shard_map/pallas_call | solution.py:523
  79.1 0.7 copy.8
  79.8 0.7 copy.9
  80.4 0.7 copy.11
Async XLA Ops:
  0.6 1.2 %copy-start = (bf16[27,128,128]{2,1,0:T(8,128)(2,1)S(1)}, bf16[27,128,128]{2,1,0:T(8,128)(2,1)}, u32[]{:S(2)}) copy-start(bf16[27,128,128]{2,1,0:T(8,128)(2,1)} %w1_h.1) | copy-start | bytes 2654212
  1.8 1.2 %copy-start.1 = (bf16[27,128,128]{2,1,0:T(8,128)(2,1)S(1)}, bf16[27,128,128]{2,1,0:T(8,128)(2,1)}, u32[]{:S(2)}) copy-start(bf16[27,128,128]{2,1,0:T(8,128)(2,1)} %w2_h.1) | copy-start | bytes 2654212
  3.0 0.9 %copy-start.2 = (bf16[1,2,32,16,128]{4,3,2,1,0:T(8,128)(2,1)S(1)}, bf16[1,2,32,16,128]{4,3,2,1,0:T(8,128)(2,1)}, u32[]{:S(2)}) copy-start(bf16[1,2,32,16,128]{4,3,2,1,0:T(8,128)(2,1)} %param.5) | copy-start | bytes 786436
  3.9 0.9 %copy-start.3 = (bf16[1,2,32,16,128]{4,3,2,1,0:T(8,128)(2,1)S(1)}, bf16[1,2,32,16,128]{4,3,2,1,0:T(8,128)(2,1)}, u32[]{:S(2)}) copy-start(bf16[1,2,32,16,128]{4,3,2,1,0:T(8,128)(2,1)} %param.6) | copy-start | bytes 786436
  4.9 0.9 %copy-start.4 = (bf16[1,2,32,16,128]{4,3,2,1,0:T(8,128)(2,1)S(1)}, bf16[1,2,32,16,128]{4,3,2,1,0:T(8,128)(2,1)}, u32[]{:S(2)}) copy-start(bf16[1,2,32,16,128]{4,3,2,1,0:T(8,128)(2,1)} %param.7) | copy-start | bytes 786436

commit v2 on v1

v2 whole, which is shorter than its diff:
```python
import functools
import math

import jax
import jax.numpy as jnp
from jax import lax
from jax.experimental import pallas as pl
from jax.experimental.pallas import tpu as pltpu
from jax.sharding import PartitionSpec as P

leak_slope = 0.3
MESH = pl.DeviceIdType.MESH
BF = jnp.bfloat16
F32 = jnp.float32

CH = 128
ROW = 16
EDGE = 32
PLANE = EDGE * ROW
PAD = PLANE + 2 * ROW
PART = PLANE // 4


def remote(src, dst, ssem, rsem, dev):
    return pltpu.make_async_remote_copy(
        src_ref=src, dst_ref=dst, send_sem=ssem, recv_sem=rsem, device_id=dev, device_id_type=MESH
    )


class Halo:
    def __init__(self, rep, g, low, high, halo, relay, ss, rs):
        self.rep, self.g = rep, g
        self.low, self.high, self.halo, self.relay, self.ss, self.rs = low, high, halo, relay, ss, rs

    def up(self):
        return remote(self.high, self.halo.at[0], self.ss.at[0], self.rs.at[0], (self.rep, self.g + 1))

    def down(self):
        return remote(self.low, self.halo.at[1], self.ss.at[1], self.rs.at[1], (self.rep, self.g - 1))

    def parts(self, side):
        src, home, first = (self.high, 3, 0) if side == 0 else (self.low, 0, 4)
        copies = []
        for k in range(4):
            rows = pl.ds(k * PART, PART)
            if k == home:
                dst, sem, dev = self.halo.at[side, rows], self.rs.at[3 + k], (self.rep, 4 - side)
            else:
                dst, sem, dev = self.relay, self.rs.at[2], (self.rep, first + k)
            copies.append(remote(src.at[rows], dst, self.ss.at[2 + k], sem, dev))
        return copies

    def pass_on(self, side):
        k = self.g if side == 0 else self.g - 4
        return remote(
            self.relay,
            self.halo.at[side, pl.ds(pl.multiple_of(k * PART, PART), PART)],
            self.ss.at[6],
            self.rs.at[3 + k],
            (self.rep, 4 - side),
        )

    def landed(self, side, k):
        block = self.halo.at[side, pl.ds(k * PART, PART)]
        return remote(block, block, self.ss.at[2 + k], self.rs.at[3 + k], (self.rep, 3 + side))

    def send_high(self):
        @pl.when((self.g != 3) & (self.g != 7))
        def _():
            self.up().start()

        @pl.when(self.g == 3)
        def _():
            for copy in self.parts(0):
                copy.start()

    def send_low(self):
        @pl.when((self.g != 0) & (self.g != 4))
        def _():
            self.down().start()

        @pl.when(self.g == 4)
        def _():
            for copy in self.parts(1):
                copy.start()

    def send(self):
        @pl.when(self.g == 4)
        def _():
            for copy in self.parts(1):
                copy.start()

        self.send_high()

        @pl.when((self.g != 0) & (self.g != 4))
        def _():
            self.down().start()

    def forward(self):
        for side, inside in ((0, self.g < 3), (1, self.g > 4)):

            @pl.when(inside)
            def _():
                copy = self.pass_on(side)
                remote(self.relay, self.relay, self.ss.at[6], self.rs.at[2], (self.rep, 4 - side)).wait_recv()
                copy.start()

    def wait_low(self):
        @pl.when((self.g != 0) & (self.g != 4))
        def _():
            self.up().wait_recv()

        @pl.when(self.g == 4)
        def _():
            for k in range(4):
                self.landed(0, k).wait_recv()

    def wait_high(self):
        @pl.when((self.g != 3) & (self.g != 7))
        def _():
            self.down().wait_recv()

        @pl.when(self.g == 3)
        def _():
            for k in range(4):
                self.landed(1, k).wait_recv()

    def drain(self):
        @pl.when((self.g != 3) & (self.g != 7))
        def _():
            self.up().wait_send()

        @pl.when((self.g != 0) & (self.g != 4))
        def _():
            self.down().wait_send()

        @pl.when(self.g == 3)
        def _():
            for copy in self.parts(0):
                copy.wait_send()

        @pl.when(self.g == 4)
        def _():
            for copy in self.parts(1):
                copy.wait_send()

        for side, inside in ((0, self.g < 3), (1, self.g > 4)):

            @pl.when(inside)
            def _():
                self.pass_on(side).wait_send()


class Where:
    def __init__(self):
        self.rep, self.g = lax.axis_index("rep"), lax.axis_index("gz")
        self.core = lax.rem(self.rep, 2)
        self.x = lax.rem(lax.div(self.rep, 2), 4)
        self.zl = lax.div(self.rep, 8)
        self.y = lax.rem(self.g, 4)
        self.zh = lax.div(self.g, 4)
        self.z = self.zh * 8 + self.zl

    def other_core(self):
        return (self.rep + 1 - 2 * self.core, self.g)

    def at_x(self, d):
        x = lax.rem(self.x + d, 4)
        return x, (self.zl * 8 + x * 2 + self.core, self.g)

    def at_y(self, d):
        y = lax.rem(self.y + d, 4)
        return y, (self.rep, self.zh * 4 + y)

    def at_z(self, d):
        z = lax.rem(self.z + d, 16)
        rest = self.rep - self.zl * 8
        return z, (lax.rem(z, 8) * 8 + rest, lax.div(z, 8) * 4 + self.y)


class Reduce:
    def __init__(self, w, s, rc, t, r1, u, r2, zs, rz, ss, rs):
        self.w = w
        self.s, self.rc, self.t, self.r1, self.u = s, rc, t, r1, u
        self.r2, self.zs, self.rz, self.ss, self.rs = r2, zs, rz, ss, rs

    def core_copy(self):
        return remote(
            self.s.at[1 - self.w.core], self.rc, self.ss.at[0], self.rs.at[0], self.w.other_core()
        )

    def first(self, half, d):
        place, dev = self.w.at_x(d) if half == 0 else self.w.at_y(d)
        k = 1 + half * 3 + d - 1
        return remote(self.t.at[half, place], self.r1.at[half, d - 1], self.ss.at[k], self.rs.at[k], dev)

    def second(self, half, d):
        place, dev = self.w.at_y(d) if half == 0 else self.w.at_x(d)
        k = 7 + half * 3 + d - 1
        return remote(self.u.at[half, place], self.r2.at[half, d - 1], self.ss.at[k], self.rs.at[k], dev)

    def last(self, d):
        place, dev = self.w.at_z(d)
        k = 13 + d - 1
        return remote(self.zs.at[place], self.rz.at[d - 1], self.ss.at[k], self.rs.at[k], dev)

    def start(self):
        self.core_copy().start()

    def step_core(self):
        self.core_copy().wait_recv()
        core = self.w.core
        for half in range(2):

            def body(i, carry):
                for j in range(4):
                    own = self.s[core, half, i, j].astype(F32)
                    self.t[half, i, j] = (own + self.rc[half, i, j].astype(F32)).astype(BF)
                return carry

            lax.fori_loop(0, 4, body, 0)
            for d in (2, 1, 3):
                self.first(half, d).start()

    def step_first(self):
        for half in range(2):
            mine = self.w.x if half == 0 else self.w.y
            for d in (1, 3, 2):
                self.first(half, d).wait_recv()

            def body(i, carry):
                total = self.t[half, mine, i].astype(F32)
                for k in range(3):
                    total += self.r1[half, k, i].astype(F32)
                self.u[half, i] = total.astype(BF)
                return carry

            lax.fori_loop(0, 4, body, 0)
            for d in (2, 1, 3):
                self.second(half, d).start()

    def step_second(self):
        for half in range(2):
            mine = self.w.y if half == 0 else self.w.x
            for d in (1, 3, 2):
                self.second(half, d).wait_recv()
            total = self.u[half, mine].astype(F32)
            for k in range(3):
                total += self.r2[half, k].astype(F32)
            self.zs[half * 8 : half * 8 + 8] = total.reshape(8, 8, CH)
        for d in (8, 7, 9, 6, 10, 5, 11, 4, 12, 3, 13, 2, 14, 1, 15):
            self.last(d).start()

    def finish(self, out, factor):
        total = self.zs[self.w.z]
        for d in (1, 15, 2, 14, 3, 13, 4, 12, 5, 11, 6, 10, 7, 9, 8):
            self.last(d).wait_recv()
            total += self.rz[d - 1]
        out[...] = total * factor

    def drain(self):
        self.core_copy().wait_send()
        for half in range(2):
            for d in (1, 2, 3):
                self.first(half, d).wait_send()
                self.second(half, d).wait_send()
        for d in range(1, 16):
            self.last(d).wait_send()


def regroup(flat, s):
    group = lax.broadcasted_iota(jnp.int32, (16, CH), 1)
    masks = {b: lax.rem(lax.div(group, 16 * b), 2) == 1 for b in (1, 2, 4)}

    def body(pair, carry):
        block = flat.at[pl.ds(pl.multiple_of(pair * 864, 8), 872)]
        rows = pl.ds(pl.multiple_of(pair * 16, 16), 16)
        for x in range(4):
            for core in range(2):
                base = x * 108 + core * 54
                v = []
                for q in range(8):
                    at = base + 7 * q
                    both = jnp.concatenate([block[at : at + 8, :], block[at + 432 : at + 440, :]], axis=0)
                    v.append(both.astype(BF))
                for b in (1, 2, 4):
                    for q in range(8):
                        if q & b:
                            continue
                        a, c = v[q], v[q | b]
                        v[q] = jnp.where(masks[b], pltpu.roll(c, 16 * b, 1), a)
                        v[q | b] = jnp.where(masks[b], c, pltpu.roll(a, CH - 16 * b, 1))
                for q in range(8):
                    if q < 4:
                        s[core, 0, x, q, rows, :] = v[q]
                    else:
                        s[core, 1, q - 4, x, rows, :] = v[q]
        return carry

    lax.fori_loop(0, 4, body, 0)


def spread(plane, ext, at):
    wide = plane.astype(F32)
    col = lax.rem(lax.broadcasted_iota(jnp.int32, (PLANE, CH), 0), ROW)
    before = jnp.where(col == 0, 0.0, pltpu.roll(wide, 1, 0)).astype(BF)
    after = jnp.where(col == ROW - 1, 0.0, pltpu.roll(wide, PLANE - 1, 0)).astype(BF)
    rows = slice(ROW, ROW + PLANE)
    ext[at, rows, 0:CH] = before
    ext[at, rows, CH : 2 * CH] = plane
    ext[at, rows, 2 * CH : 3 * CH] = after


def slabs(ext, at):
    return jnp.concatenate([ext[at, dy * ROW : dy * ROW + PLANE, :] for dy in range(3)], axis=1)


def mm(a, b):
    return jnp.dot(a, b, preferred_element_type=F32)


def lay_weights(w, wt):
    for a in range(3):
        for dy in range(3):
            for dx in range(3):
                k = dy * 3 + dx
                wt[a, k * CH : (k + 1) * CH, :] = w[9 * a + 8 - k].T


def inner_data_grad(ext, wt, acc):
    for at in (1, 2):
        x = slabs(ext, at)
        pair = jnp.concatenate([wt[2 - at], wt[3 - at]], axis=1)
        if at == 1:
            acc[...] = mm(x, pair)
        else:
            acc[...] += mm(x, pair)


def kernel(
    factor, li_h, pa_h, ct_h, w1_h, w2_h, ig, tiles,
    li, pa, ct, w1, w2, ig_v, ct_halo, li_halo, pg_halo, ct_relay, li_relay, pg_relay,
    e_ct, e_pg, pg, act_t, li_t, wt2, wt1, acc, flat1, flat2,
    s1, rc1, t1, r11, u1, r21, zs1, rz1, s2, rc2, t2, r12, u2, r22, zs2, rz2,
    in_sem, hs_ct, hr_ct, hs_li, hr_li, hs_pg, hr_pg, ss1, rs1, ss2, rs2,
):
    w = Where()
    rep, g = w.rep, w.g
    loads = [
        pltpu.make_async_copy(a, b, in_sem.at[k])
        for k, (a, b) in enumerate([(ct_h, ct), (w2_h, w2), (pa_h, pa), (li_h, li), (w1_h, w1)])
    ]
    for load in loads:
        load.start()

    barrier = pltpu.get_barrier_semaphore()
    peers = [w.other_core()]
    peers += [w.at_x(d)[1] for d in (1, 2, 3)] + [w.at_y(d)[1] for d in (1, 2, 3)]
    peers += [w.at_z(d)[1] for d in range(1, 16)]
    for dev in peers:
        pl.semaphore_signal(barrier, inc=1, device_id=dev, device_id_type=MESH)
    for end, senders in ((3, (4, 5, 6)), (4, (1, 2, 3))):

        @pl.when(g == end)
        def _():
            for k in senders:
                pl.semaphore_signal(barrier, inc=1, device_id=(rep, k), device_id_type=MESH)

    @pl.when(g == 0)
    def _():
        for halo in (ct_halo, li_halo, pg_halo):
            halo[0] = jnp.zeros((PLANE, CH), BF)

    @pl.when(g == 7)
    def _():
        for halo in (ct_halo, li_halo, pg_halo):
            halo[1] = jnp.zeros((PLANE, CH), BF)

    edge = jnp.zeros((4, ROW, 3 * CH), BF)
    for ext in (e_ct, e_pg):
        ext[:, 0:ROW, :] = edge
        ext[:, ROW + PLANE : PAD, :] = edge
    for flat in (flat1, flat2):
        flat[27 * CH : 27 * CH + 8, :] = jnp.zeros((8, CH), F32)
    loads[0].wait()

    between = (g > 0) & (g < 7)

    @pl.when(between)
    def _():
        pl.semaphore_wait(barrier, len(peers) + 1)

    @pl.when(jnp.logical_not(between))
    def _():
        pl.semaphore_wait(barrier, len(peers))

    low, high = pl.ds(0, PLANE), pl.ds(PLANE, PLANE)
    h_ct = Halo(rep, g, ct.at[low], ct.at[high], ct_halo, ct_relay, hs_ct, hr_ct)
    h_li = Halo(rep, g, li.at[low], li.at[high], li_halo, li_relay, hs_li, hr_li)
    h_pg = Halo(rep, g, pg.at[low], pg.at[high], pg_halo, pg_relay, hs_pg, hr_pg)
    red1 = Reduce(w, s1, rc1, t1, r11, u1, r21, zs1, rz1, ss1, rs1)
    red2 = Reduce(w, s2, rc2, t2, r12, u2, r22, zs2, rz2, ss2, rs2)
    h_ct.send()
    spread(ct[low, :], e_ct, 1)
    spread(ct[high, :], e_ct, 2)
    loads[1].wait()
    lay_weights(w2, wt2)
    h_ct.forward()
    loads[3].wait()
    h_li.send()
    inner_data_grad(e_ct, wt2, acc)
    loads[2].wait()
    for q in range(2):
        v = pa[q * PLANE : (q + 1) * PLANE, :].astype(F32)
        act = jnp.where(v > 0, v, leak_slope * v).astype(BF)
        act_t[:, q * PLANE : (q + 1) * PLANE] = act.T
    li_t[:, PLANE : 2 * PLANE] = li[low, :].T
    li_t[:, 2 * PLANE : 3 * PLANE] = li[high, :].T
    h_li.forward()

    order = [(0, 1), (2, 3), (4, 5), (6, 7), (8,)]

    def taps(ext, at, group):
        parts = []
        for k in group:
            dy, dx = 2 - k // 3, 2 - k % 3
            parts.append(ext[at, dy * ROW : dy * ROW + PLANE, dx * CH : (dx + 1) * CH])
        return parts[0] if len(parts) == 1 else jnp.concatenate(parts, axis=1)

    def put(flat, group, a, value, more=False):
        for j, k in enumerate(group):
            t = 9 * a + k
            rows = slice(t * CH, (t + 1) * CH)
            tap = value[:, j * CH : (j + 1) * CH]
            flat[rows, :] = flat[rows, :] + tap if more else tap

    a0, a1 = act_t[:, 0:PLANE], act_t[:, PLANE : 2 * PLANE]
    for group in order:
        stack = jnp.concatenate([a0, a1], axis=0)
        mid = mm(stack, taps(e_ct, 1, group))
        after = mm(stack, taps(e_ct, 2, group))
        put(flat2, group, 0, after[:CH])
        put(flat2, group, 1, mid[:CH] + after[CH:])
        put(flat2, group, 2, mid[CH:])
    loads[4].wait()
    lay_weights(w1, wt1)

    for q in range(2):
        if q == 0:
            h_ct.wait_low()
        else:
            h_ct.wait_high()
        spread(ct_halo[q], e_ct, 3 * q)
        total = acc[:, q * CH : (q + 1) * CH] + mm(slabs(e_ct, 3 * q), wt2[2 - 2 * q])
        rows = pl.ds(q * PLANE, PLANE)
        v = pa[rows, :].astype(F32)
        pg[rows, :] = (total * jnp.where(v > 0, 1.0, leak_slope)).astype(BF)
        if q == 0:
            h_pg.send_low()
        else:
            h_pg.send_high()

    def edge_two():
        for group in order:
            put(flat2, group, 0, mm(a1, taps(e_ct, 3, group)), more=True)
            put(flat2, group, 2, mm(a0, taps(e_ct, 0, group)), more=True)

    def send_two():
        regroup(flat2, s2)
        red2.start()

    def spread_pg():
        spread(pg[low, :], e_pg, 1)
        spread(pg[high, :], e_pg, 2)

    def turn_li():
        h_li.wait_low()
        li_t[:, 0:PLANE] = li_halo[0].T
        h_li.wait_high()
        li_t[:, 3 * PLANE : 4 * PLANE] = li_halo[1].T

    def grad_one():
        for group in order:
            total = None
            for at in (1, 2):
                lhs = jnp.concatenate(
                    [li_t[:, (at + a - 1) * PLANE : (at + a) * PLANE] for a in range(3)], axis=0
                )
                term = mm(lhs, taps(e_pg, at, group))
                total = term if total is None else total + term
            for a in range(3):
                put(flat1, group, a, total[a * CH : (a + 1) * CH])

    def send_one():
        regroup(flat1, s1)
        red1.start()

    def inner():
        inner_data_grad(e_pg, wt1, acc)

    def pg_low():
        h_pg.wait_low()
        spread(pg_halo[0], e_pg, 0)

    def pg_high():
        h_pg.wait_high()
        spread(pg_halo[1], e_pg, 3)

    save = pltpu.make_async_copy(ig_v, ig, in_sem.at[5])

    def outer():
        for q in range(2):
            total = acc[:, q * CH : (q + 1) * CH] + mm(slabs(e_pg, 3 * q), wt1[2 - 2 * q])
            ig_v[q * PLANE : (q + 1) * PLANE, :] = total.astype(BF)
        save.start()

    steps = (edge_two, send_two, h_pg.forward, spread_pg, turn_li, grad_one, red2.step_core, send_one, inner, red1.step_core, red2.step_first, pg_low, pg_high, outer, red1.step_first, red2.step_second, red1.step_second, functools.partial(red2.finish, tiles.at[1], factor), functools.partial(red1.finish, tiles.at[0], factor))
    for step in steps:
        step()
    save.wait()

    for halo in (h_ct, h_li, h_pg):
        halo.drain()
    red2.drain()
    red1.drain()


def close(ig_in, tiles, ig, one, two, through, load_sem, save_sem):
    rows = ig_in.shape[0] // 4
    loads, saves = [], []
    for k in range(4):
        at = pl.ds(k * rows, rows)
        loads.append(pltpu.make_async_copy(ig_in.at[at], through.at[at], load_sem.at[k]))
        saves.append(pltpu.make_async_copy(through.at[at], ig.at[at], save_sem.at[k]))
        loads[k].start()
    for k in range(4):
        loads[k].wait()
        saves[k].start()
    for k, out in enumerate((one, two)):
        turned = tiles[k].T
        for q in range(8):
            rows = 7 if q < 7 else 5
            out[:, 7 * q : 7 * q + rows] = turned[16 * q : 16 * q + 16, :rows]
    for save in saves:
        save.wait()


def reduce_buffers():
    return [
        pltpu.VMEM((2, 2, 4, 4, 64, CH), BF),
        pltpu.VMEM((2, 4, 4, 64, CH), BF),
        pltpu.VMEM((2, 4, 4, 64, CH), BF),
        pltpu.VMEM((2, 3, 4, 64, CH), BF),
        pltpu.VMEM((2, 4, 64, CH), BF),
        pltpu.VMEM((2, 3, 64, CH), BF),
        pltpu.VMEM((16, 8, CH), F32),
        pltpu.VMEM((15, 8, CH), F32),
    ]


def on_device(layer_input, pre_act, cotangent, w_one, w_two):
    shape = layer_input.shape
    cells = 2 * PLANE
    factor = 1.0 / math.sqrt(cells * lax.axis_size("rep") * lax.axis_size("gz"))
    flat_in = [v.reshape(cells, CH) for v in (layer_input, pre_act, cotangent)]
    any_spec = pl.BlockSpec(memory_space=pl.ANY)
    vmem_spec = pl.BlockSpec(memory_space=pltpu.VMEM)
    dma = pltpu.SemaphoreType.DMA
    field = pltpu.VMEM((cells, CH), BF)
    kern = pltpu.VMEM((27, CH, CH), BF)
    halo = pltpu.VMEM((2, PLANE, CH), BF)
    relay = pltpu.VMEM((PART, CH), BF)
    ext = pltpu.VMEM((4, PAD, 3 * CH), BF)
    turned = pltpu.VMEM((3, 9 * CH, CH), BF)
    held, tiles = pl.pallas_call(
        functools.partial(kernel, factor),
        out_shape=(
            jax.ShapeDtypeStruct((cells, CH), BF),
            jax.ShapeDtypeStruct((2, 8, CH), F32),
        ),
        in_specs=[any_spec] * 5,
        out_specs=(any_spec, vmem_spec),
        scratch_shapes=[
            field, field, field, kern, kern, field, halo, halo, halo, relay, relay, relay,
            ext, ext, field, pltpu.VMEM((CH, cells), BF), pltpu.VMEM((CH, 2 * cells), BF),
            turned, turned, pltpu.VMEM((PLANE, 2 * CH), F32), *[pltpu.VMEM((27 * CH + 8, CH), F32)] * 2,
            *reduce_buffers(), *reduce_buffers(),
            dma((6,)), *[dma((7,))] * 6, *[dma((28,))] * 4,
        ],
        compiler_params=pltpu.CompilerParams(
            collective_id=0, has_side_effects=True, vmem_limit_bytes=62 * 2**20
        ),
    )(*flat_in, w_one, w_two)
    input_grad, one, two = pl.pallas_call(
        close,
        out_shape=(
            jax.ShapeDtypeStruct((cells, CH), BF),
            jax.ShapeDtypeStruct((16, 54), F32),
            jax.ShapeDtypeStruct((16, 54), F32),
        ),
        in_specs=[any_spec, vmem_spec],
        out_specs=(any_spec, vmem_spec, vmem_spec),
        scratch_shapes=[field, dma((4,)), dma((4,))],
    )(held, tiles)
    return (input_grad.reshape(shape), one.T, two.T)


def solution(mesh):
    cells = P("rep", "gz", None, None, None)
    return jax.shard_map(
        on_device,
        mesh=mesh,
        in_specs=(cells, cells, cells, P(), P()),
        out_specs=(cells, P("rep", "gz"), P("rep", "gz")),
        check_vma=False,
    )
```

time: 81.4 us -> 63.2 us (0.78)
  Pallas kernels: 73.3 us -> 62.2 us
  local copies, waits for them, and re-layouts: 7.22 us -> 0 us
    pallas_call x1, Pallas kernels: 73.3 us -> 59.2 us  [on_device(): pl.pallas_call(functools.partial(kernel, factor), out_shape=(jax.ShapeDty...]
    unnamed x13 -> x0, local copies, waits for them, and re-layouts: 7.22 us -> none
    pallas_call x0 -> x1, Pallas kernels: none -> 2.93 us  [on_device(): pl.pallas_call(close, out_shape=(jax.ShapeDtypeStruct((cells, CH), BF), j...]
where the time goes in v2:
time: 63.2 us; the launch traced here: 62.8 us
  Pallas kernels  62.2 us (98%)
  between operations  0.64 us (1%)
    pallas_call x1, Pallas kernels, on_device(): pl.pallas_call(functools.partial(kernel, factor), out_shape=(jax.ShapeDty...  59.2 us
    pallas_call x1, Pallas kernels, on_device(): pl.pallas_call(close, out_shape=(jax.ShapeDtypeStruct((cells, CH), BF), j...  2.93 us

profile of v2, /device:TPU:32, one launch (start us, length us, event | category | flops | bytes accessed | tf_op | source)
XLA Modules:
  0.0 62.8 jit_solution(9476900338545515099)
XLA Ops:
  0.6 59.2 %shard_map.76 = (bf16[1024,128]{1,0:T(8,128)(2,1)}, f32[2,8,128]{2,1,0:T(8,128)}) custom-call(bf16[1024,128]{1,0:T(8,128)(2,1)} %bitcast.6, bf16[1024,128]{1,0:T(8,128)(2,1)} %bitcast.7, bf16[1024,128]{1,0:T(8,128)(2,1)} %bitcast.8, bf16[27,128,128]{2,1,0:T(8,128)(2,1)} %w1_h.1, bf16[27,128,128]{2,1,0:T(8,128)(2,1)} %w2_h.1), custom_call_target="tpu_custom_call" | custom-call | tf_op jit(solution)/shard_map/pallas_call | solution.py:575
  59.9 2.9 %shard_map.77 = (bf16[1024,128]{1,0:T(8,128)(2,1)}, f32[16,54]{1,0:T(8,128)}, f32[16,54]{1,0:T(8,128)}) custom-call(bf16[1024,128]{1,0:T(8,128)(2,1)} %get-tuple-element.8.ig_in, f32[2,8,128]{2,1,0:T(8,128)} %get-tuple-element.9.tiles), custom_call_target="tpu_custom_call" | custom-call | tf_op jit(solution)/shard_map/pallas_call | solution.py:594

commit v3 on v2

--- a/solution.py
+++ b/solution.py
@@ -184,97 +184,121 @@
         self.s, self.rc, self.t, self.r1, self.u = s, rc, t, r1, u
         self.r2, self.zs, self.rz, self.ss, self.rs = r2, zs, rz, ss, rs
 
-    def core_copy(self):
+    def core_copy(self, half):
         return remote(
-            self.s.at[1 - self.w.core], self.rc, self.ss.at[0], self.rs.at[0], self.w.other_core()
+            self.s.at[1 - self.w.core, half],
+            self.rc.at[half],
+            self.ss.at[half],
+            self.rs.at[half],
+            self.w.other_core(),
         )
 
     def first(self, half, d):
         place, dev = self.w.at_x(d) if half == 0 else self.w.at_y(d)
-        k = 1 + half * 3 + d - 1
+        k = 2 + half * 3 + d - 1
         return remote(self.t.at[half, place], self.r1.at[half, d - 1], self.ss.at[k], self.rs.at[k], dev)
 
     def second(self, half, d):
         place, dev = self.w.at_y(d) if half == 0 else self.w.at_x(d)
-        k = 7 + half * 3 + d - 1
+        k = 8 + half * 3 + d - 1
         return remote(self.u.at[half, place], self.r2.at[half, d - 1], self.ss.at[k], self.rs.at[k], dev)
 
-    def last(self, d):
-        place, dev = self.w.at_z(d)
-        k = 13 + d - 1
-        return remote(self.zs.at[place], self.rz.at[d - 1], self.ss.at[k], self.rs.at[k], dev)
-
-    def start(self):
-        self.core_copy().start()
-
-    def step_core(self):
-        self.core_copy().wait_recv()
+    def chunk(self, zl, zh):
+        within = lax.rem(zl, 4)
+        return lax.div(within, 2) * 4 + zh * 2 + lax.rem(within, 2)
+
+    def last(self, half):
+        w = self.w
+        copies = []
+        for flip in (1, 0):
+            zh = 1 - w.zh if flip else w.zh
+            for k in (2, 1, 3, 0):
+                zl = half * 4 + lax.rem(w.zl + k, 4)
+                dev = (zl * 8 + w.rep - w.zl * 8, zh * 4 + w.y)
+                copy = remote(
+                    self.zs.at[half, self.chunk(zl, zh)],
+                    self.rz.at[w.z],
+                    self.ss.at[14 + half * 8 + flip * 4 + k],
+                    self.rs.at[14 + w.z],
+                    dev,
+                )
+                copies.append((flip == 1 or k > 0, copy))
+        return copies
+
+    def each_last(self, half, act):
+        for always, copy in self.last(half):
+            if always:
+                act(copy)
+            else:
+
+                @pl.when(lax.div(self.w.zl, 4) != half)
+                def _():
+                    act(copy)
+
+    def step_core(self, half):
+        self.core_copy(half).wait_recv()
         core = self.w.core
+
+        def body(i, carry):
+            for j in range(4):
+                own = self.s[core, half, i, j].astype(F32)
+                self.t[half, i, j] = (own + self.rc[half, i, j].astype(F32)).astype(BF)
+            return carry
+
+        lax.fori_loop(0, 4, body, 0)
+        for d in (2, 1, 3):
+            self.first(half, d).start()
+
+    def step_first(self, half):
+        mine = self.w.x if half == 0 else self.w.y
+        for d in (1, 3, 2):
+            self.first(half, d).wait_recv()
+
+        def body(i, carry):
+            total = self.t[half, mine, i].astype(F32)
+            for k in range(3):
+                total += self.r1[half, k, i].astype(F32)
+            self.u[half, i] = total.astype(BF)
+            return carry
+
+        lax.fori_loop(0, 4, body, 0)
+        for d in (2, 1, 3):
+            self.second(half, d).start()
+
+    def step_second(self, half):
+        mine = self.w.y if half == 0 else self.w.x
+        for d in (1, 3, 2):
+            self.second(half, d).wait_recv()
+        total = self.u[half, mine].astype(F32)
+        for k in range(3):
+            total += self.r2[half, k].astype(F32)
+        self.zs[half] = total.reshape(8, 8, CH)
+        self.each_last(half, lambda copy: copy.start())
+
+    def finish(self, out, factor):
+        w = self.w
+        total = self.zs[lax.div(w.zl, 4), self.chunk(w.zl, w.zh)]
+        for d in (1, 15, 2, 14, 3, 13, 4, 12, 5, 11, 6, 10, 7, 9, 8):
+            z, dev = w.at_z(d)
+            remote(self.zs.at[0, 0], self.rz.at[z], self.ss.at[14], self.rs.at[14 + z], dev).wait_recv()
+            total += self.rz[z]
+        out[...] = total * factor
+
+    def drain(self):
         for half in range(2):
-
-            def body(i, carry):
-                for j in range(4):
-                    own = self.s[core, half, i, j].astype(F32)
-                    self.t[half, i, j] = (own + self.rc[half, i, j].astype(F32)).astype(BF)
-                return carry
-
-            lax.fori_loop(0, 4, body, 0)
-            for d in (2, 1, 3):
-                self.first(half, d).start()
-
-    def step_first(self):
-        for half in range(2):
-            mine = self.w.x if half == 0 else self.w.y
-            for d in (1, 3, 2):
-                self.first(half, d).wait_recv()
-
-            def body(i, carry):
-                total = self.t[half, mine, i].astype(F32)
-                for k in range(3):
-                    total += self.r1[half, k, i].astype(F32)
-                self.u[half, i] = total.astype(BF)
-                return carry
-
-            lax.fori_loop(0, 4, body, 0)
-            for d in (2, 1, 3):
-                self.second(half, d).start()
-
-    def step_second(self):
-        for half in range(2):
-            mine = self.w.y if half == 0 else self.w.x
-            for d in (1, 3, 2):
-                self.second(half, d).wait_recv()
-            total = self.u[half, mine].astype(F32)
-            for k in range(3):
-                total += self.r2[half, k].astype(F32)
-            self.zs[half * 8 : half * 8 + 8] = total.reshape(8, 8, CH)
-        for d in (8, 7, 9, 6, 10, 5, 11, 4, 12, 3, 13, 2, 14, 1, 15):
-            self.last(d).start()
-
-    def finish(self, out, factor):
-        total = self.zs[self.w.z]
-        for d in (1, 15, 2, 14, 3, 13, 4, 12, 5, 11, 6, 10, 7, 9, 8):
-            self.last(d).wait_recv()
-            total += self.rz[d - 1]
-        out[...] = total * factor
-
-    def drain(self):
-        self.core_copy().wait_send()
-        for half in range(2):
+            self.core_copy(half).wait_send()
             for d in (1, 2, 3):
                 self.first(half, d).wait_send()
                 self.second(half, d).wait_send()
-        for d in range(1, 16):
-            self.last(d).wait_send()
-
-
-def regroup(flat, s):
+            self.each_last(half, lambda copy: copy.wait_send())
+
+
+def regroup(flat, s, half):
     group = lax.broadcasted_iota(jnp.int32, (16, CH), 1)
     masks = {b: lax.rem(lax.div(group, 16 * b), 2) == 1 for b in (1, 2, 4)}
 
     def body(pair, carry):
-        block = flat.at[pl.ds(pl.multiple_of(pair * 864, 8), 872)]
-        rows = pl.ds(pl.multiple_of(pair * 16, 16), 16)
+        block = flat.at[pl.ds(pl.multiple_of((half * 2 + pair) * 864, 8), 872)]
         for x in range(4):
             for core in range(2):
                 base = x * 108 + core * 54
@@ -291,13 +315,14 @@
                         v[q] = jnp.where(masks[b], pltpu.roll(c, 16 * b, 1), a)
                         v[q | b] = jnp.where(masks[b], c, pltpu.roll(a, CH - 16 * b, 1))
                 for q in range(8):
-                    if q < 4:
-                        s[core, 0, x, q, rows, :] = v[q]
+                    rows = pl.ds(pl.multiple_of(pair * 32 + (q // 4) * 16, 16), 16)
+                    if half == 0:
+                        s[core, 0, x, q % 4, rows, :] = v[q]
                     else:
-                        s[core, 1, q - 4, x, rows, :] = v[q]
+                        s[core, 1, q % 4, x, rows, :] = v[q]
         return carry
 
-    lax.fori_loop(0, 4, body, 0)
+    lax.fori_loop(0, 2, body, 0)
 
 
 def spread(plane, ext, at):
@@ -346,13 +371,6 @@
 ):
     w = Where()
     rep, g = w.rep, w.g
-    loads = [
-        pltpu.make_async_copy(a, b, in_sem.at[k])
-        for k, (a, b) in enumerate([(ct_h, ct), (w2_h, w2), (pa_h, pa), (li_h, li), (w1_h, w1)])
-    ]
-    for load in loads:
-        load.start()
-
     barrier = pltpu.get_barrier_semaphore()
     peers = [w.other_core()]
     peers += [w.at_x(d)[1] for d in (1, 2, 3)] + [w.at_y(d)[1] for d in (1, 2, 3)]
@@ -365,6 +383,13 @@
         def _():
             for k in senders:
                 pl.semaphore_signal(barrier, inc=1, device_id=(rep, k), device_id_type=MESH)
+
+    loads = [
+        pltpu.make_async_copy(a, b, in_sem.at[k])
+        for k, (a, b) in enumerate([(ct_h, ct), (w2_h, w2), (pa_h, pa), (li_h, li), (w1_h, w1)])
+    ]
+    for load in loads:
+        load.start()
 
     @pl.when(g == 0)
     def _():
@@ -466,8 +491,9 @@
             put(flat2, group, 2, mm(a0, taps(e_ct, 0, group)), more=True)
 
     def send_two():
-        regroup(flat2, s2)
-        red2.start()
+        for half in (0, 1):
+            regroup(flat2, s2, half)
+            red2.core_copy(half).start()
 
     def spread_pg():
         spread(pg[low, :], e_pg, 1)
@@ -492,8 +518,9 @@
                 put(flat1, group, a, total[a * CH : (a + 1) * CH])
 
     def send_one():
-        regroup(flat1, s1)
-        red1.start()
+        for half in (0, 1):
+            regroup(flat1, s1, half)
+            red1.core_copy(half).start()
 
     def inner():
         inner_data_grad(e_pg, wt1, acc)
@@ -514,9 +541,31 @@
             ig_v[q * PLANE : (q + 1) * PLANE, :] = total.astype(BF)
         save.start()
 
-    steps = (edge_two, send_two, h_pg.forward, spread_pg, turn_li, grad_one, red2.step_core, send_one, inner, red1.step_core, red2.step_first, pg_low, pg_high, outer, red1.step_first, red2.step_second, red1.step_second, functools.partial(red2.finish, tiles.at[1], factor), functools.partial(red1.finish, tiles.at[0], factor))
-    for step in steps:
-        step()
+    edge_two()
+    send_two()
+    h_pg.forward()
+    spread_pg()
+    turn_li()
+    grad_one()
+    red2.step_core(0)
+    red2.step_core(1)
+    send_one()
+    inner()
+    red1.step_core(0)
+    red1.step_core(1)
+    red2.step_first(0)
+    red2.step_first(1)
+    pg_low()
+    pg_high()
+    outer()
+    red1.step_first(0)
+    red1.step_first(1)
+    red2.step_second(0)
+    red2.step_second(1)
+    red1.step_second(0)
+    red1.step_second(1)
+    red2.finish(tiles.at[1], factor)
+    red1.finish(tiles.at[0], factor)
     save.wait()
 
     for halo in (h_ct, h_li, h_pg):
@@ -525,7 +574,9 @@
     red1.drain()
 
 
-def close(ig_in, tiles, ig, one, two, through, load_sem, save_sem):
+def close(ig_in, tiles_in, ig, one, two, through, tiles, turned, load_sem, save_sem):
+    small = pltpu.make_async_copy(tiles_in, tiles, load_sem.at[4])
+    small.start()
     rows = ig_in.shape[0] // 4
     loads, saves = [], []
     for k in range(4):
@@ -533,14 +584,17 @@
         loads.append(pltpu.make_async_copy(ig_in.at[at], through.at[at], load_sem.at[k]))
         saves.append(pltpu.make_async_copy(through.at[at], ig.at[at], save_sem.at[k]))
         loads[k].start()
+    small.wait()
+    for k, out in enumerate((one, two)):
+        flip = tiles[k].T
+        for q in range(8):
+            size = 7 if q < 7 else 5
+            turned[k, :, 7 * q : 7 * q + size] = flip[16 * q : 16 * q + 16, :size]
+        saves.append(pltpu.make_async_copy(turned.at[k], out, save_sem.at[4 + k]))
+        saves[4 + k].start()
     for k in range(4):
         loads[k].wait()
         saves[k].start()
-    for k, out in enumerate((one, two)):
-        turned = tiles[k].T
-        for q in range(8):
-            rows = 7 if q < 7 else 5
-            out[:, 7 * q : 7 * q + rows] = turned[16 * q : 16 * q + 16, :rows]
     for save in saves:
         save.wait()
 
@@ -553,8 +607,8 @@
         pltpu.VMEM((2, 3, 4, 64, CH), BF),
         pltpu.VMEM((2, 4, 64, CH), BF),
         pltpu.VMEM((2, 3, 64, CH), BF),
+        pltpu.VMEM((2, 8, 8, CH), F32),
         pltpu.VMEM((16, 8, CH), F32),
-        pltpu.VMEM((15, 8, CH), F32),
     ]
 
 
@@ -585,7 +639,7 @@
             ext, ext, field, pltpu.VMEM((CH, cells), BF), pltpu.VMEM((CH, 2 * cells), BF),
             turned, turned, pltpu.VMEM((PLANE, 2 * CH), F32), *[pltpu.VMEM((27 * CH + 8, CH), F32)] * 2,
             *reduce_buffers(), *reduce_buffers(),
-            dma((6,)), *[dma((7,))] * 6, *[dma((28,))] * 4,
+            dma((6,)), *[dma((7,))] * 6, *[dma((30,))] * 4,
         ],
         compiler_params=pltpu.CompilerParams(
             collective_id=0, has_side_effects=True, vmem_limit_bytes=62 * 2**20
@@ -598,9 +652,11 @@
             jax.ShapeDtypeStruct((16, 54), F32),
             jax.ShapeDtypeStruct((16, 54), F32),
         ),
-        in_specs=[any_spec, vmem_spec],
-        out_specs=(any_spec, vmem_spec, vmem_spec),
-        scratch_shapes=[field, dma((4,)), dma((4,))],
+        in_specs=[any_spec, any_spec],
+        out_specs=(any_spec, any_spec, any_spec),
+        scratch_shapes=[
+            field, pltpu.VMEM((2, 8, CH), F32), pltpu.VMEM((2, 16, 54), F32), dma((5,)), dma((6,)),
+        ],
     )(held, tiles)
     return (input_grad.reshape(shape), one.T, two.T)
 

time: 63.2 us -> 61 us (0.965)
  Pallas kernels: 62.2 us -> 60.2 us
    pallas_call x1, Pallas kernels: 2.93 us -> 1.68 us  [on_device(): pl.pallas_call(close, out_shape=(jax.ShapeDtypeStruct((cells, CH), BF), j...]
    pallas_call x1, Pallas kernels: 59.2 us -> 58.5 us  [on_device(): pl.pallas_call(functools.partial(kernel, factor), out_shape=(jax.ShapeDty...]
where the time goes in v3:
time: 61 us; the launch traced here: 60.8 us
  Pallas kernels  60.2 us (99%)
  between operations  0.64 us (1%)
    pallas_call x1, Pallas kernels, on_device(): pl.pallas_call(functools.partial(kernel, factor), out_shape=(jax.ShapeDty...  58.5 us
    pallas_call x1, Pallas kernels, on_device(): pl.pallas_call(close, out_shape=(jax.ShapeDtypeStruct((cells, CH), BF), j...  1.68 us

profile of v3, /device:TPU:32, one launch (start us, length us, event | category | flops | bytes accessed | tf_op | source)
XLA Modules:
  0.0 60.8 jit_solution(13094816636702054296)
XLA Ops:
  0.6 58.5 %shard_map.76 = (bf16[1024,128]{1,0:T(8,128)(2,1)}, f32[2,8,128]{2,1,0:T(8,128)}) custom-call(bf16[1024,128]{1,0:T(8,128)(2,1)} %bitcast.6, bf16[1024,128]{1,0:T(8,128)(2,1)} %bitcast.7, bf16[1024,128]{1,0:T(8,128)(2,1)} %bitcast.8, bf16[27,128,128]{2,1,0:T(8,128)(2,1)} %w1_h.1, bf16[27,128,128]{2,1,0:T(8,128)(2,1)} %w2_h.1), custom_call_target="tpu_custom_call" | custom-call | tf_op jit(solution)/shard_map/pallas_call | solution.py:629
  59.1 1.7 %shard_map.77 = (bf16[1024,128]{1,0:T(8,128)(2,1)}, f32[16,54]{1,0:T(8,128)}, f32[16,54]{1,0:T(8,128)}) custom-call(bf16[1024,128]{1,0:T(8,128)(2,1)} %get-tuple-element.8.ig_in, f32[2,8,128]{2,1,0:T(8,128)} %get-tuple-element.9.tiles_in), custom_call_target="tpu_custom_call" | custom-call | tf_op jit(solution)/shard_map/pallas_call | solution.py:648

commit v4 on v3

--- a/solution.py
+++ b/solution.py
@@ -356,10 +356,10 @@
     for at in (1, 2):
         x = slabs(ext, at)
         pair = jnp.concatenate([wt[2 - at], wt[3 - at]], axis=1)
-        if at == 1:
-            acc[...] = mm(x, pair)
-        else:
-            acc[...] += mm(x, pair)
+        both = mm(x, pair)
+        for q in range(2):
+            part = both[:, q * CH : (q + 1) * CH]
+            acc[q] = part if at == 1 else acc[q] + part
 
 
 def kernel(
@@ -374,7 +374,8 @@
     barrier = pltpu.get_barrier_semaphore()
     peers = [w.other_core()]
     peers += [w.at_x(d)[1] for d in (1, 2, 3)] + [w.at_y(d)[1] for d in (1, 2, 3)]
-    peers += [w.at_z(d)[1] for d in range(1, 16)]
+    far_first = (8, 7, 9, 6, 10, 5, 11, 4, 12, 3, 13, 2, 14, 1, 15)
+    peers = [w.at_z(d)[1] for d in far_first] + peers
     for dev in peers:
         pl.semaphore_signal(barrier, inc=1, device_id=dev, device_id_type=MESH)
     for end, senders in ((3, (4, 5, 6)), (4, (1, 2, 3))):
@@ -438,9 +439,9 @@
     for q in range(2):
         v = pa[q * PLANE : (q + 1) * PLANE, :].astype(F32)
         act = jnp.where(v > 0, v, leak_slope * v).astype(BF)
-        act_t[:, q * PLANE : (q + 1) * PLANE] = act.T
-    li_t[:, PLANE : 2 * PLANE] = li[low, :].T
-    li_t[:, 2 * PLANE : 3 * PLANE] = li[high, :].T
+        act_t[q] = act.T
+    li_t[1] = li[low, :].T
+    li_t[2] = li[high, :].T
     h_li.forward()
 
     order = [(0, 1), (2, 3), (4, 5), (6, 7), (8,)]
@@ -455,13 +456,12 @@
     def put(flat, group, a, value, more=False):
         for j, k in enumerate(group):
             t = 9 * a + k
-            rows = slice(t * CH, (t + 1) * CH)
+            rows = pl.ds(pl.multiple_of(t * CH, CH), CH)
             tap = value[:, j * CH : (j + 1) * CH]
             flat[rows, :] = flat[rows, :] + tap if more else tap
 
-    a0, a1 = act_t[:, 0:PLANE], act_t[:, PLANE : 2 * PLANE]
     for group in order:
-        stack = jnp.concatenate([a0, a1], axis=0)
+        stack = jnp.concatenate([act_t[0], act_t[1]], axis=0)
         mid = mm(stack, taps(e_ct, 1, group))
         after = mm(stack, taps(e_ct, 2, group))
         put(flat2, group, 0, after[:CH])
@@ -470,57 +470,59 @@
     loads[4].wait()
     lay_weights(w1, wt1)
 
-    for q in range(2):
-        if q == 0:
+    near = lax.div(g, 4)
+
+    def pre_grad(q):
+        @pl.when(q == 0)
+        def _():
             h_ct.wait_low()
-        else:
+
+        @pl.when(q == 1)
+        def _():
             h_ct.wait_high()
+
         spread(ct_halo[q], e_ct, 3 * q)
-        total = acc[:, q * CH : (q + 1) * CH] + mm(slabs(e_ct, 3 * q), wt2[2 - 2 * q])
-        rows = pl.ds(q * PLANE, PLANE)
+        total = acc[q] + mm(slabs(e_ct, 3 * q), wt2[2 - 2 * q])
+        rows = pl.ds(pl.multiple_of(q * PLANE, PLANE), PLANE)
         v = pa[rows, :].astype(F32)
-        pg[rows, :] = (total * jnp.where(v > 0, 1.0, leak_slope)).astype(BF)
-        if q == 0:
+        own = (total * jnp.where(v > 0, 1.0, leak_slope)).astype(BF)
+        pg[rows, :] = own
+        spread(own, e_pg, 1 + q)
+
+        @pl.when(q == 0)
+        def _():
             h_pg.send_low()
-        else:
+
+        @pl.when(q == 1)
+        def _():
             h_pg.send_high()
 
-    def edge_two():
+    def edge_two(q):
         for group in order:
-            put(flat2, group, 0, mm(a1, taps(e_ct, 3, group)), more=True)
-            put(flat2, group, 2, mm(a0, taps(e_ct, 0, group)), more=True)
-
-    def send_two():
+            put(flat2, group, 2 - 2 * q, mm(act_t[q], taps(e_ct, 3 * q, group)), more=True)
+
+    def turn_li(q):
+        @pl.when(q == 0)
+        def _():
+            h_li.wait_low()
+
+        @pl.when(q == 1)
+        def _():
+            h_li.wait_high()
+
+        li_t[3 * q] = li_halo[q].T
+
+    def grad_one(q, more):
+        for group in order:
+            lhs = jnp.concatenate([li_t[q + a] for a in range(3)], axis=0)
+            total = mm(lhs, taps(e_pg, 1 + q, group))
+            for a in range(3):
+                put(flat1, group, a, total[a * CH : (a + 1) * CH], more)
+
+    def send(flat, s, red):
         for half in (0, 1):
-            regroup(flat2, s2, half)
-            red2.core_copy(half).start()
-
-    def spread_pg():
-        spread(pg[low, :], e_pg, 1)
-        spread(pg[high, :], e_pg, 2)
-
-    def turn_li():
-        h_li.wait_low()
-        li_t[:, 0:PLANE] = li_halo[0].T
-        h_li.wait_high()
-        li_t[:, 3 * PLANE : 4 * PLANE] = li_halo[1].T
-
-    def grad_one():
-        for group in order:
-            total = None
-            for at in (1, 2):
-                lhs = jnp.concatenate(
-                    [li_t[:, (at + a - 1) * PLANE : (at + a) * PLANE] for a in range(3)], axis=0
-                )
-                term = mm(lhs, taps(e_pg, at, group))
-                total = term if total is None else total + term
-            for a in range(3):
-                put(flat1, group, a, total[a * CH : (a + 1) * CH])
-
-    def send_one():
-        for half in (0, 1):
-            regroup(flat1, s1, half)
-            red1.core_copy(half).start()
+            regroup(flat, s, half)
+            red.core_copy(half).start()
 
     def inner():
         inner_data_grad(e_pg, wt1, acc)
@@ -537,19 +539,23 @@
 
     def outer():
         for q in range(2):
-            total = acc[:, q * CH : (q + 1) * CH] + mm(slabs(e_pg, 3 * q), wt1[2 - 2 * q])
+            total = acc[q] + mm(slabs(e_pg, 3 * q), wt1[2 - 2 * q])
             ig_v[q * PLANE : (q + 1) * PLANE, :] = total.astype(BF)
         save.start()
 
-    edge_two()
-    send_two()
+    pre_grad(near)
+    edge_two(near)
+    turn_li(near)
+    grad_one(near, False)
+    pre_grad(1 - near)
+    edge_two(1 - near)
+    send(flat2, s2, red2)
     h_pg.forward()
-    spread_pg()
-    turn_li()
-    grad_one()
+    turn_li(1 - near)
+    grad_one(1 - near, True)
     red2.step_core(0)
     red2.step_core(1)
-    send_one()
+    send(flat1, s1, red1)
     inner()
     red1.step_core(0)
     red1.step_core(1)
@@ -636,8 +642,8 @@
         out_specs=(any_spec, vmem_spec),
         scratch_shapes=[
             field, field, field, kern, kern, field, halo, halo, halo, relay, relay, relay,
-            ext, ext, field, pltpu.VMEM((CH, cells), BF), pltpu.VMEM((CH, 2 * cells), BF),
-            turned, turned, pltpu.VMEM((PLANE, 2 * CH), F32), *[pltpu.VMEM((27 * CH + 8, CH), F32)] * 2,
+            ext, ext, field, pltpu.VMEM((2, CH, PLANE), BF), pltpu.VMEM((4, CH, PLANE), BF),
+            turned, turned, pltpu.VMEM((2, PLANE, CH), F32), *[pltpu.VMEM((27 * CH + 8, CH), F32)] * 2,
             *reduce_buffers(), *reduce_buffers(),
             dma((6,)), *[dma((7,))] * 6, *[dma((30,))] * 4,
         ],

time: 61 us -> 58.7 us (0.962)
  the two profiles are of different devices: /device:TPU:32 before, /device:TPU:8 now
where the time goes in v4:
time: 58.7 us; the launch traced here: 58.5 us
  Pallas kernels  57.9 us (99%)
  between operations  0.64 us (1%)
    pallas_call x1, Pallas kernels, on_device(): pl.pallas_call(functools.partial(kernel, factor), out_shape=(jax.ShapeDty...  56.2 us
    pallas_call x1, Pallas kernels, on_device(): pl.pallas_call(close, out_shape=(jax.ShapeDtypeStruct((cells, CH), BF), j...  1.68 us

profile of v4, /device:TPU:8, one launch (start us, length us, event | category | flops | bytes accessed | tf_op | source)
XLA Modules:
  0.0 58.5 jit_solution(1372526040109983264)
XLA Ops:
  0.6 56.2 %shard_map.76 = (bf16[1024,128]{1,0:T(8,128)(2,1)}, f32[2,8,128]{2,1,0:T(8,128)}) custom-call(bf16[1024,128]{1,0:T(8,128)(2,1)} %bitcast.6, bf16[1024,128]{1,0:T(8,128)(2,1)} %bitcast.7, bf16[1024,128]{1,0:T(8,128)(2,1)} %bitcast.8, bf16[27,128,128]{2,1,0:T(8,128)(2,1)} %w1_h.1, bf16[27,128,128]{2,1,0:T(8,128)(2,1)} %w2_h.1), custom_call_target="tpu_custom_call" | custom-call | tf_op jit(solution)/shard_map/pallas_call | solution.py:635
  56.8 1.7 %shard_map.77 = (bf16[1024,128]{1,0:T(8,128)(2,1)}, f32[16,54]{1,0:T(8,128)}, f32[16,54]{1,0:T(8,128)}) custom-call(bf16[1024,128]{1,0:T(8,128)(2,1)} %get-tuple-element.8.ig_in, f32[2,8,128]{2,1,0:T(8,128)} %get-tuple-element.9.tiles_in), custom_call_target="tpu_custom_call" | custom-call | tf_op jit(solution)/shard_map/pallas_call | solution.py:654

commit v5 on v4

--- a/solution.py
+++ b/solution.py
@@ -293,12 +293,13 @@
             self.each_last(half, lambda copy: copy.wait_send())
 
 
-def regroup(flat, s, half):
+def regroup(flat, s, red):
     group = lax.broadcasted_iota(jnp.int32, (16, CH), 1)
     masks = {b: lax.rem(lax.div(group, 16 * b), 2) == 1 for b in (1, 2, 4)}
 
-    def body(pair, carry):
-        block = flat.at[pl.ds(pl.multiple_of((half * 2 + pair) * 864, 8), 872)]
+    def body(step, carry):
+        half, pair = lax.div(step, 2), lax.rem(step, 2)
+        block = flat.at[pl.ds(pl.multiple_of(step * 864, 8), 872)]
         for x in range(4):
             for core in range(2):
                 base = x * 108 + core * 54
@@ -316,13 +317,16 @@
                         v[q | b] = jnp.where(masks[b], c, pltpu.roll(a, CH - 16 * b, 1))
                 for q in range(8):
                     rows = pl.ds(pl.multiple_of(pair * 32 + (q // 4) * 16, 16), 16)
-                    if half == 0:
-                        s[core, 0, x, q % 4, rows, :] = v[q]
-                    else:
-                        s[core, 1, q % 4, x, rows, :] = v[q]
+                    y = q % 4
+                    s[core, half, x + half * (y - x), y + half * (x - y), rows, :] = v[q]
+
+        @pl.when(pair == 1)
+        def _():
+            red.core_copy(half).start()
+
         return carry
 
-    lax.fori_loop(0, 2, body, 0)
+    lax.fori_loop(0, 4, body, 0)
 
 
 def spread(plane, ext, at):
@@ -345,11 +349,12 @@
 
 
 def lay_weights(w, wt):
-    for a in range(3):
-        for dy in range(3):
-            for dx in range(3):
-                k = dy * 3 + dx
-                wt[a, k * CH : (k + 1) * CH, :] = w[9 * a + 8 - k].T
+    def body(a, carry):
+        for k in range(9):
+            wt[a, k * CH : (k + 1) * CH, :] = w[9 * a + 8 - k].T
+        return carry
+
+    lax.fori_loop(0, 3, body, 0)
 
 
 def inner_data_grad(ext, wt, acc):
@@ -467,8 +472,6 @@
         put(flat2, group, 0, after[:CH])
         put(flat2, group, 1, mid[:CH] + after[CH:])
         put(flat2, group, 2, mid[CH:])
-    loads[4].wait()
-    lay_weights(w1, wt1)
 
     near = lax.div(g, 4)
 
@@ -520,9 +523,7 @@
                 put(flat1, group, a, total[a * CH : (a + 1) * CH], more)
 
     def send(flat, s, red):
-        for half in (0, 1):
-            regroup(flat, s, half)
-            red.core_copy(half).start()
+        regroup(flat, s, red)
 
     def inner():
         inner_data_grad(e_pg, wt1, acc)
@@ -556,6 +557,8 @@
     red2.step_core(0)
     red2.step_core(1)
     send(flat1, s1, red1)
+    loads[4].wait()
+    lay_weights(w1, wt1)
     inner()
     red1.step_core(0)
     red1.step_core(1)
@@ -570,14 +573,14 @@
     red2.step_second(1)
     red1.step_second(0)
     red1.step_second(1)
-    red2.finish(tiles.at[1], factor)
-    red1.finish(tiles.at[0], factor)
     save.wait()
 
     for halo in (h_ct, h_li, h_pg):
         halo.drain()
     red2.drain()
     red1.drain()
+    red2.finish(tiles.at[1], factor)
+    red1.finish(tiles.at[0], factor)
 
 
 def close(ig_in, tiles_in, ig, one, two, through, tiles, turned, load_sem, save_sem):

time: 58.7 us -> 58.6 us (level)
  the two profiles are of different devices: /device:TPU:8 before, /device:TPU:32 now
where the time goes in v5:
time: 58.6 us; the launch traced here: 58.1 us
  Pallas kernels  57.5 us (98%)
  between operations  0.64 us (1%)
    pallas_call x1, Pallas kernels, on_device(): pl.pallas_call(functools.partial(kernel, factor), out_shape=(jax.ShapeDty...  55.8 us
    pallas_call x1, Pallas kernels, on_device(): pl.pallas_call(close, out_shape=(jax.ShapeDtypeStruct((cells, CH), BF), j...  1.68 us

profile of v5, /device:TPU:32, one launch (start us, length us, event | category | flops | bytes accessed | tf_op | source)
XLA Modules:
  0.0 58.1 jit_solution(8264457349588648312)
XLA Ops:
  0.6 55.8 %shard_map.76 = (bf16[1024,128]{1,0:T(8,128)(2,1)}, f32[2,8,128]{2,1,0:T(8,128)}) custom-call(bf16[1024,128]{1,0:T(8,128)(2,1)} %bitcast.6, bf16[1024,128]{1,0:T(8,128)(2,1)} %bitcast.7, bf16[1024,128]{1,0:T(8,128)(2,1)} %bitcast.8, bf16[27,128,128]{2,1,0:T(8,128)(2,1)} %w1_h.1, bf16[27,128,128]{2,1,0:T(8,128)(2,1)} %w2_h.1), custom_call_target="tpu_custom_call" | custom-call | tf_op jit(solution)/shard_map/pallas_call | solution.py:638
  56.5 1.7 %shard_map.77 = (bf16[1024,128]{1,0:T(8,128)(2,1)}, f32[16,54]{1,0:T(8,128)}, f32[16,54]{1,0:T(8,128)}) custom-call(bf16[1024,128]{1,0:T(8,128)(2,1)} %get-tuple-element.8.ig_in, f32[2,8,128]{2,1,0:T(8,128)} %get-tuple-element.9.tiles_in), custom_call_target="tpu_custom_call" | custom-call | tf_op jit(solution)/shard_map/pallas_call | solution.py:657

commit v6 on v5

--- a/solution.py
+++ b/solution.py
@@ -413,7 +413,6 @@
         ext[:, ROW + PLANE : PAD, :] = edge
     for flat in (flat1, flat2):
         flat[27 * CH : 27 * CH + 8, :] = jnp.zeros((8, CH), F32)
-    loads[0].wait()
 
     between = (g > 0) & (g < 7)
 
@@ -426,12 +425,13 @@
         pl.semaphore_wait(barrier, len(peers))
 
     low, high = pl.ds(0, PLANE), pl.ds(PLANE, PLANE)
-    h_ct = Halo(rep, g, ct.at[low], ct.at[high], ct_halo, ct_relay, hs_ct, hr_ct)
-    h_li = Halo(rep, g, li.at[low], li.at[high], li_halo, li_relay, hs_li, hr_li)
+    h_ct = Halo(rep, g, ct_h.at[low], ct_h.at[high], ct_halo, ct_relay, hs_ct, hr_ct)
+    h_li = Halo(rep, g, li_h.at[low], li_h.at[high], li_halo, li_relay, hs_li, hr_li)
     h_pg = Halo(rep, g, pg.at[low], pg.at[high], pg_halo, pg_relay, hs_pg, hr_pg)
     red1 = Reduce(w, s1, rc1, t1, r11, u1, r21, zs1, rz1, ss1, rs1)
     red2 = Reduce(w, s2, rc2, t2, r12, u2, r22, zs2, rz2, ss2, rs2)
     h_ct.send()
+    loads[0].wait()
     spread(ct[low, :], e_ct, 1)
     spread(ct[high, :], e_ct, 2)
     loads[1].wait()

time: 58.6 us -> 58.8 us (level)
  the two profiles are of different devices: /device:TPU:32 before, /device:TPU:8 now
where the time goes in v6:
time: 58.8 us; the launch traced here: 58.6 us
  Pallas kernels  58 us (99%)
  between operations  0.64 us (1%)
    pallas_call x1, Pallas kernels, on_device(): pl.pallas_call(functools.partial(kernel, factor), out_shape=(jax.ShapeDty...  56.3 us
    pallas_call x1, Pallas kernels, on_device(): pl.pallas_call(close, out_shape=(jax.ShapeDtypeStruct((cells, CH), BF), j...  1.68 us

profile of v6, /device:TPU:8, one launch (start us, length us, event | category | flops | bytes accessed | tf_op | source)
XLA Modules:
  0.0 58.6 jit_solution(8354756059893516966)
XLA Ops:
  0.6 56.3 %shard_map.76 = (bf16[1024,128]{1,0:T(8,128)(2,1)}, f32[2,8,128]{2,1,0:T(8,128)}) custom-call(bf16[1024,128]{1,0:T(8,128)(2,1)} %bitcast.6, bf16[1024,128]{1,0:T(8,128)(2,1)} %bitcast.7, bf16[1024,128]{1,0:T(8,128)(2,1)} %bitcast.8, bf16[27,128,128]{2,1,0:T(8,128)(2,1)} %w1_h.1, bf16[27,128,128]{2,1,0:T(8,128)(2,1)} %w2_h.1), custom_call_target="tpu_custom_call" | custom-call | tf_op jit(solution)/shard_map/pallas_call | solution.py:638
  56.9 1.7 %shard_map.77 = (bf16[1024,128]{1,0:T(8,128)(2,1)}, f32[16,54]{1,0:T(8,128)}, f32[16,54]{1,0:T(8,128)}) custom-call(bf16[1024,128]{1,0:T(8,128)(2,1)} %get-tuple-element.8.ig_in, f32[2,8,128]{2,1,0:T(8,128)} %get-tuple-element.9.tiles_in), custom_call_target="tpu_custom_call" | custom-call | tf_op jit(solution)/shard_map/pallas_call | solution.py:657
